TPU v7x, 32 devices: a whole 2x2x4 slice. The times are simulated.
32 devices in a mesh: dp: 4 (over y, x), seq: 8 (over z, core).
Axes of the slice: x: 2, y: 2, z: 4, core: 2. Of those that a mesh axis runs over, the one named last changes fastest.
Arguments:
- long_frames: bfloat16 [8, 640, 1024], P('dp', 'seq'), may hold values from -6 to 6
- short_frames: bfloat16 [8, 512, 1024], P('dp', 'seq'), may hold values from -6 to 6
- long_text: bfloat16 [8, 64, 768], P('dp'), may hold values from -6 to 6
- short_text: bfloat16 [8, 64, 768], P('dp'), may hold values from -6 to 6
- long_lengths: int32 [8], P('dp'), may hold values from 320 to 640, as said below
- short_lengths: int32 [8], P('dp'), may hold values from 256 to 512, as said below
- text_lengths: int32 [2, 8], P(None, 'dp'), may hold values from 32 to 64, as said below
- qkv_weight: bfloat16 [1024, 3072], P('seq'), may hold values from -0.1875 to 0.1875
- self_out: bfloat16 [1024, 1024], P('seq'), may hold values from -1.5 to 1.5
- cross_query: bfloat16 [1024, 1024], P('seq'), may hold values from -0.1875 to 0.1875
- cross_keyval: bfloat16 [1024, 2048], P('seq'), may hold values from -0.1875 to 0.1875
- cross_out: bfloat16 [1024, 1024], P('seq'), may hold values from -0.75 to 0.75
- text_proj: bfloat16 [768, 1024], P('seq'), may hold values from -0.21875 to 0.21875
- text_bias: bfloat16 [1024], P('seq'), may hold values from -3 to 3
- feed_in: bfloat16 [1024, 4096], P('seq'), may hold values from -0.1875 to 0.1875
- feed_out: bfloat16 [4096, 1024], P('seq'), may hold values from -0.09375 to 0.09375
- norm_gains: bfloat16 [3, 1024], P(None, 'seq'), may hold values from 0.5 to 1.5
- norm_shifts: bfloat16 [3, 1024], P(None, 'seq'), may hold values from -2 to 2
- long_cot: bfloat16 [8, 640, 1024], P('dp', 'seq'), may hold values from -6 to 6
- short_cot: bfloat16 [8, 512, 1024], P('dp', 'seq'), may hold values from -6 to 6
Outputs:
- long_output: bfloat16 [8, 640, 1024], P('dp', 'seq')
- short_output: bfloat16 [8, 512, 1024], P('dp', 'seq')
- long_input_grad: float32 [8, 640, 1024], P('dp', 'seq')
- short_input_grad: float32 [8, 512, 1024], P('dp', 'seq')
- long_text_grad: float32 [8, 64, 768], P('dp', 'seq')
- short_text_grad: float32 [8, 64, 768], P('dp', 'seq')
- qkv_grad: float32 [1024, 3072], P('seq')
- self_out_grad: float32 [1024, 1024], P('seq')
- cross_query_grad: float32 [1024, 1024], P('seq')
- cross_keyval_grad: float32 [1024, 2048], P('seq')
- cross_out_grad: float32 [1024, 1024], P('seq')
- text_proj_grad: float32 [768, 1024], P('seq')
- text_bias_grad: float32 [1024], P('seq')
- feed_in_grad: float32 [1024, 4096], P('seq')
- feed_out_grad: float32 [4096, 1024], P('seq')
- gains_grad: float32 [3, 1024], P(None, 'seq')
- shifts_grad: float32 [3, 1024], P(None, 'seq')
Inputs may be any that keep to these rules, and one draw needn't show every extreme that they name: `long_lengths`: frames of a long item at or past its length are padding that no frame attends to; in every draw some long item has all 640. `short_lengths`: frames of a short item at or past its length are padding that no frame attends to; in every draw some short item has all 512. `text_lengths`: an item's frames attend to its first that many text states; in each row some item has all 64.
All inputs are finite; a program needn't handle non-finite values.
Results may differ from a plain program's by a relative error of at most 0.025.
Values may be sent and summed in bfloat16 or wider, within the bound.
No kernel may reach another device: no remote copies, remote signals or barrier semaphores. Data moves between devices by JAX's collectives and lax.ppermute only.
A program may use at most 256 MiB of HBM per device.

v0:
```python
from functools import partial

import jax
import jax.numpy as jnp
from jax import lax
from jax.sharding import PartitionSpec as P

D = 1024
HEADS = 16
ENC = 768
TEXT = 64


masked_value = -1e30
norm_eps = 1e-05


def layer_norm(values, gain_row, bias_row):
    average = jnp.mean(values, -1, keepdims=True)
    centred = values - average
    spread = jnp.mean(centred * centred, -1, keepdims=True)
    return centred * lax.rsqrt(spread + norm_eps) * gain_row + bias_row


def norm_back(values, gain_row, bias_row, incoming):
    _, pullback = jax.vjp(layer_norm, values, gain_row, bias_row)
    return pullback(incoming)


def product(left, right):
    return jnp.dot(left, right, preferred_element_type=jnp.float32)


def product_t(left, right):
    return lax.dot_general(
        left, right, (((left.ndim - 1,), (1,)), ((), ())), preferred_element_type=jnp.float32
    )


def weight_grad(left, right):
    return lax.dot_general(
        left, right, (((0,), (0,)), ((), ())), preferred_element_type=jnp.float32
    )


def head_view(packed, head_dim):
    return packed.reshape(packed.shape[0], packed.shape[1], -1, head_dim)


def flatten_heads(tensor):
    return tensor.reshape(tensor.shape[0], tensor.shape[1], -1).astype(jnp.bfloat16)


def softmax_weights(query, keys, mask, score_scale):
    scores = (
        jnp.einsum("iqhd,ikhd->ihqk", query, keys, preferred_element_type=jnp.float32) * score_scale
    )
    scores = jnp.where(mask, scores, masked_value)
    row_max = jnp.max(scores, -1, keepdims=True)
    raised = jnp.exp(scores - row_max)
    return raised / jnp.sum(raised, -1, keepdims=True)


def attend_forward(query, keys, values, mask, score_scale):
    weights = softmax_weights(query, keys, mask, score_scale).astype(jnp.bfloat16)
    mixed = jnp.einsum("ihqk,ikhd->iqhd", weights, values, preferred_element_type=jnp.float32)
    return flatten_heads(mixed)


def attend_backward(query, keys, values, mask, score_scale, grad_out):
    probs = softmax_weights(query, keys, mask, score_scale)
    grad_values = jnp.einsum(
        "ihqk,iqhd->ikhd", probs.astype(jnp.bfloat16), grad_out, preferred_element_type=jnp.float32
    )
    grad_probs = jnp.einsum("iqhd,ikhd->ihqk", grad_out, values, preferred_element_type=jnp.float32)
    centre = jnp.sum(probs * grad_probs, -1, keepdims=True)
    grad_scores = (probs * (grad_probs - centre)).astype(jnp.bfloat16)
    grad_query = (
        jnp.einsum("ihqk,ikhd->iqhd", grad_scores, keys, preferred_element_type=jnp.float32)
        * score_scale
    )
    grad_keys = (
        jnp.einsum("ihqk,iqhd->ikhd", grad_scores, query, preferred_element_type=jnp.float32)
        * score_scale
    )
    return (flatten_heads(grad_query), flatten_heads(grad_keys), flatten_heads(grad_values))


def on_device(
    long_frames,
    short_frames,
    long_text,
    short_text,
    long_lengths,
    short_lengths,
    text_lengths,
    qkv_weight,
    self_out,
    cross_query,
    cross_keyval,
    cross_out,
    text_proj,
    text_bias,
    feed_in,
    feed_out,
    norm_gains,
    norm_shifts,
    long_cot,
    short_cot,
):
    w_qkv, w_self, w_query, w_keyval, w_cross, w_text, b_text, w_in, w_out, gains, shifts = (
        lax.all_gather(qkv_weight, "seq", axis=0, tiled=True),
        lax.all_gather(self_out, "seq", axis=0, tiled=True),
        lax.all_gather(cross_query, "seq", axis=0, tiled=True),
        lax.all_gather(cross_keyval, "seq", axis=0, tiled=True),
        lax.all_gather(cross_out, "seq", axis=0, tiled=True),
        lax.all_gather(text_proj, "seq", axis=0, tiled=True),
        lax.all_gather(text_bias, "seq", axis=0, tiled=True),
        lax.all_gather(feed_in, "seq", axis=0, tiled=True),
        lax.all_gather(feed_out, "seq", axis=0, tiled=True),
        lax.all_gather(norm_gains, "seq", axis=1, tiled=True),
        lax.all_gather(norm_shifts, "seq", axis=1, tiled=True),
    )
    seq_count = lax.axis_size("seq")
    seq_rank = lax.axis_index("seq")
    head_dim = D // HEADS
    head_width = D // seq_count
    score_scale = head_dim ** (-0.5)
    item_count, long_rows, _ = long_frames.shape
    short_rows = short_frames.shape[1]
    long_total = item_count * long_rows
    long_len = long_rows * seq_count
    short_len = short_rows * seq_count

    def to_items(joined):
        last_dim = joined.shape[-1]
        return (
            joined[:long_total].reshape(item_count, long_rows, last_dim),
            joined[long_total:].reshape(item_count, short_rows, last_dim),
        )

    def to_rows(long_part, short_part):
        return jnp.concatenate(
            [
                long_part.reshape(long_part.shape[0] * long_part.shape[1], -1),
                short_part.reshape(short_part.shape[0] * short_part.shape[1], -1),
            ],
            0,
        )

    def self_mask(lengths, full):
        places = jnp.arange(full)
        causal = places[:, None] >= places[None, :]
        return causal[None, None] & (places[None, None, None, :] < lengths[:, None, None, None])

    def text_mask(lengths):
        places = jnp.arange(TEXT)
        return (places[None, :] < lengths[:, None])[:, None, None, :]

    def split_three(packed):
        return (
            head_view(packed[:, :, 0], head_dim),
            head_view(packed[:, :, 1], head_dim),
            head_view(packed[:, :, 2], head_dim),
        )

    masks_self = (self_mask(long_lengths, long_len), self_mask(short_lengths, short_len))
    masks_text = (text_mask(text_lengths[0]), text_mask(text_lengths[1]))
    inputs = to_rows(long_frames, short_frames).astype(jnp.float32)
    normed_self = layer_norm(inputs, gains[0], shifts[0]).astype(jnp.bfloat16)

    def self_heads():
        packed = product(normed_self, w_qkv).astype(jnp.bfloat16)
        long_part, short_part = to_items(packed)
        long_part = long_part.reshape(item_count, long_rows, 3, D)
        short_part = short_part.reshape(item_count, short_rows, 3, D)
        return (
            lax.all_to_all(long_part, "seq", split_axis=3, concat_axis=1, tiled=True),
            lax.all_to_all(short_part, "seq", split_axis=3, concat_axis=1, tiled=True),
        )

    heads_pair = self_heads()
    long_mixed = attend_forward(*split_three(heads_pair[0]), masks_self[0], score_scale)
    short_mixed = attend_forward(*split_three(heads_pair[1]), masks_self[1], score_scale)
    long_back, short_back = (
        lax.all_to_all(long_mixed, "seq", split_axis=1, concat_axis=2, tiled=True),
        lax.all_to_all(short_mixed, "seq", split_axis=1, concat_axis=2, tiled=True),
    )
    self_rows = to_rows(long_back, short_back)
    after_self = inputs + product(self_rows, w_self)
    normed_cross = layer_norm(after_self, gains[1], shifts[1]).astype(jnp.bfloat16)
    long_query, short_query = to_items(product(normed_cross, w_query).astype(jnp.bfloat16))
    query_heads = (
        lax.all_to_all(long_query, "seq", split_axis=2, concat_axis=1, tiled=True),
        lax.all_to_all(short_query, "seq", split_axis=2, concat_axis=1, tiled=True),
    )
    key_cols = lax.dynamic_slice_in_dim(w_keyval, seq_rank * head_width, head_width, 1)
    value_cols = lax.dynamic_slice_in_dim(w_keyval, D + seq_rank * head_width, head_width, 1)
    texts = (long_text, short_text)
    encoded = tuple(((product(words, w_text) + b_text).astype(jnp.bfloat16) for words in texts))
    text_keys = tuple((product(enc_rows, key_cols).astype(jnp.bfloat16) for enc_rows in encoded))
    text_values = tuple(
        (product(enc_rows, value_cols).astype(jnp.bfloat16) for enc_rows in encoded)
    )
    cross_long = attend_forward(
        head_view(query_heads[0], head_dim),
        head_view(text_keys[0], head_dim),
        head_view(text_values[0], head_dim),
        masks_text[0],
        score_scale,
    )
    cross_short = attend_forward(
        head_view(query_heads[1], head_dim),
        head_view(text_keys[1], head_dim),
        head_view(text_values[1], head_dim),
        masks_text[1],
        score_scale,
    )
    cross_back_long, cross_back_short = (
        lax.all_to_all(cross_long, "seq", split_axis=1, concat_axis=2, tiled=True),
        lax.all_to_all(cross_short, "seq", split_axis=1, concat_axis=2, tiled=True),
    )
    cross_rows = to_rows(cross_back_long, cross_back_short)
    after_cross = after_self + product(cross_rows, w_cross)
    normed_feed = layer_norm(after_cross, gains[2], shifts[2]).astype(jnp.bfloat16)
    pre_act = product(normed_feed, w_in)
    hidden = jax.nn.gelu(pre_act, approximate=False).astype(jnp.bfloat16)
    result = after_cross + product(hidden, w_out)
    grad_rows = to_rows(long_cot, short_cot)
    feed_out_grad = weight_grad(hidden, grad_rows)
    _, gelu_pull = jax.vjp(partial(jax.nn.gelu, approximate=False), pre_act)
    grad_pre = gelu_pull(product_t(grad_rows, w_out))[0].astype(jnp.bfloat16)
    feed_in_grad = weight_grad(normed_feed, grad_pre)
    grad_cross_in, gain_two, shift_two = norm_back(
        after_cross, gains[2], shifts[2], product_t(grad_pre, w_in)
    )
    grad_after_cross = grad_rows.astype(jnp.float32) + grad_cross_in
    cross_branch = grad_after_cross.astype(jnp.bfloat16)
    cross_out_grad = weight_grad(cross_rows, cross_branch)
    long_dco, short_dco = to_items(product_t(cross_branch, w_cross).astype(jnp.bfloat16))
    grad_heads = (
        lax.all_to_all(long_dco, "seq", split_axis=2, concat_axis=1, tiled=True),
        lax.all_to_all(short_dco, "seq", split_axis=2, concat_axis=1, tiled=True),
    )
    cross_parts = tuple(
        (
            attend_backward(
                head_view(query_heads[bucket], head_dim),
                head_view(text_keys[bucket], head_dim),
                head_view(text_values[bucket], head_dim),
                masks_text[bucket],
                score_scale,
                head_view(grad_heads[bucket], head_dim),
            )
            for bucket in range(2)
        )
    )
    long_dq, short_dq = (
        lax.all_to_all(cross_parts[0][0], "seq", split_axis=1, concat_axis=2, tiled=True),
        lax.all_to_all(cross_parts[1][0], "seq", split_axis=1, concat_axis=2, tiled=True),
    )
    query_rows = to_rows(long_dq, short_dq)
    cross_query_grad = weight_grad(normed_cross, query_rows)
    grad_self_in, gain_one, shift_one = norm_back(
        after_self, gains[1], shifts[1], product_t(query_rows, w_query)
    )
    grad_after_self = grad_after_cross + grad_self_in
    key_grad = jnp.zeros((D, head_width), jnp.float32)
    value_grad = jnp.zeros((D, head_width), jnp.float32)
    for bucket in range(2):
        key_grad = key_grad + jnp.einsum(
            "itd,itw->dw",
            encoded[bucket],
            cross_parts[bucket][1],
            preferred_element_type=jnp.float32,
        )
        value_grad = value_grad + jnp.einsum(
            "itd,itw->dw",
            encoded[bucket],
            cross_parts[bucket][2],
            preferred_element_type=jnp.float32,
        )
    keyval_grad = jnp.zeros((D, 2 * D), jnp.float32)
    keyval_grad = lax.dynamic_update_slice_in_dim(keyval_grad, key_grad, seq_rank * head_width, 1)
    keyval_grad = lax.dynamic_update_slice_in_dim(
        keyval_grad, value_grad, D + seq_rank * head_width, 1
    )
    enc_long = product_t(cross_parts[0][1], key_cols) + product_t(cross_parts[0][2], value_cols)
    enc_short = product_t(cross_parts[1][1], key_cols) + product_t(cross_parts[1][2], value_cols)
    summed_long, summed_short = (
        lax.psum_scatter(
            enc_long.astype(jnp.bfloat16), "seq", scatter_dimension=1, tiled=True
        ).astype(jnp.float32),
        lax.psum_scatter(
            enc_short.astype(jnp.bfloat16), "seq", scatter_dimension=1, tiled=True
        ).astype(jnp.float32),
    )
    enc_grads = (summed_long.astype(jnp.bfloat16), summed_short.astype(jnp.bfloat16))
    text_rows = TEXT // seq_count
    own_text = tuple(
        (lax.dynamic_slice_in_dim(words, seq_rank * text_rows, text_rows, 1) for words in texts)
    )
    text_grads = tuple((product_t(enc_grad, w_text) for enc_grad in enc_grads))
    text_proj_grad = jnp.zeros((ENC, D), jnp.float32)
    text_bias_grad = jnp.zeros((D,), jnp.float32)
    for bucket in range(2):
        text_proj_grad = text_proj_grad + jnp.einsum(
            "ite,itd->ed", own_text[bucket], enc_grads[bucket], preferred_element_type=jnp.float32
        )
        text_bias_grad = text_bias_grad + jnp.sum(enc_grads[bucket].astype(jnp.float32), (0, 1))
    self_branch = grad_after_self.astype(jnp.bfloat16)
    self_out_grad = weight_grad(self_rows, self_branch)
    long_do, short_do = to_items(product_t(self_branch, w_self).astype(jnp.bfloat16))
    out_heads = (
        lax.all_to_all(long_do, "seq", split_axis=2, concat_axis=1, tiled=True),
        lax.all_to_all(short_do, "seq", split_axis=2, concat_axis=1, tiled=True),
    )
    kept_heads = self_heads()
    self_parts = tuple(
        (
            attend_backward(
                *split_three(kept_heads[bucket]),
                masks_self[bucket],
                score_scale,
                head_view(out_heads[bucket], head_dim)
            )
            for bucket in range(2)
        )
    )
    stacked_long = jnp.stack(self_parts[0], 2)
    stacked_short = jnp.stack(self_parts[1], 2)
    long_qkv, short_qkv = (
        lax.all_to_all(stacked_long, "seq", split_axis=1, concat_axis=3, tiled=True),
        lax.all_to_all(stacked_short, "seq", split_axis=1, concat_axis=3, tiled=True),
    )
    qkv_rows = to_rows(long_qkv, short_qkv)
    qkv_grad = weight_grad(normed_self, qkv_rows)
    grad_first, gain_zero, shift_zero = norm_back(
        inputs, gains[0], shifts[0], product_t(qkv_rows, w_qkv)
    )
    input_grad = grad_after_self + grad_first
    grads = (
        qkv_grad,
        self_out_grad,
        cross_query_grad,
        keyval_grad,
        cross_out_grad,
        text_proj_grad,
        text_bias_grad,
        feed_in_grad,
        feed_out_grad,
        jnp.stack([gain_zero, gain_one, gain_two]),
        jnp.stack([shift_zero, shift_one, shift_two]),
    )
    shares = (
        lax.psum_scatter(
            grads[0].astype(jnp.bfloat16), "seq", scatter_dimension=0, tiled=True
        ).astype(jnp.float32),
        lax.psum_scatter(
            grads[1].astype(jnp.bfloat16), "seq", scatter_dimension=0, tiled=True
        ).astype(jnp.float32),
        lax.psum_scatter(
            grads[2].astype(jnp.bfloat16), "seq", scatter_dimension=0, tiled=True
        ).astype(jnp.float32),
        lax.psum_scatter(
            grads[3].astype(jnp.bfloat16), "seq", scatter_dimension=0, tiled=True
        ).astype(jnp.float32),
        lax.psum_scatter(
            grads[4].astype(jnp.bfloat16), "seq", scatter_dimension=0, tiled=True
        ).astype(jnp.float32),
        lax.psum_scatter(
            grads[5].astype(jnp.bfloat16), "seq", scatter_dimension=0, tiled=True
        ).astype(jnp.float32),
        lax.psum_scatter(
            grads[6].astype(jnp.bfloat16), "seq", scatter_dimension=0, tiled=True
        ).astype(jnp.float32),
        lax.psum_scatter(
            grads[7].astype(jnp.bfloat16), "seq", scatter_dimension=0, tiled=True
        ).astype(jnp.float32),
        lax.psum_scatter(
            grads[8].astype(jnp.bfloat16), "seq", scatter_dimension=0, tiled=True
        ).astype(jnp.float32),
        lax.psum_scatter(grads[9], "seq", scatter_dimension=1, tiled=True).astype(jnp.float32),
        lax.psum_scatter(grads[10], "seq", scatter_dimension=1, tiled=True).astype(jnp.float32),
    )
    totals = (
        lax.psum(shares[0].astype(jnp.bfloat16), "dp").astype(jnp.float32),
        lax.psum(shares[1].astype(jnp.bfloat16), "dp").astype(jnp.float32),
        lax.psum(shares[2].astype(jnp.bfloat16), "dp").astype(jnp.float32),
        lax.psum(shares[3].astype(jnp.bfloat16), "dp").astype(jnp.float32),
        lax.psum(shares[4].astype(jnp.bfloat16), "dp").astype(jnp.float32),
        lax.psum(shares[5].astype(jnp.bfloat16), "dp").astype(jnp.float32),
        lax.psum(shares[6].astype(jnp.bfloat16), "dp").astype(jnp.float32),
        lax.psum(shares[7].astype(jnp.bfloat16), "dp").astype(jnp.float32),
        lax.psum(shares[8].astype(jnp.bfloat16), "dp").astype(jnp.float32),
        lax.psum(shares[9].astype(jnp.bfloat16), "dp").astype(jnp.float32),
        lax.psum(shares[10].astype(jnp.bfloat16), "dp").astype(jnp.float32),
    )
    long_output, short_output = to_items(result.astype(jnp.bfloat16))
    long_input_grad, short_input_grad = to_items(input_grad)
    return (
        long_output,
        short_output,
        long_input_grad,
        short_input_grad,
        text_grads[0],
        text_grads[1],
        totals[0],
        totals[1],
        totals[2],
        totals[3],
        totals[4],
        totals[5],
        totals[6],
        totals[7],
        totals[8],
        totals[9],
        totals[10],
    )


def solution(mesh):
    return jax.shard_map(
        on_device,
        mesh=mesh,
        in_specs=(
            P("dp", "seq", None),
            P("dp", "seq", None),
            P("dp", None, None),
            P("dp", None, None),
            P("dp"),
            P("dp"),
            P(None, "dp"),
            P("seq", None),
            P("seq", None),
            P("seq", None),
            P("seq", None),
            P("seq", None),
            P("seq", None),
            P("seq"),
            P("seq", None),
            P("seq", None),
            P(None, "seq"),
            P(None, "seq"),
            P("dp", "seq", None),
            P("dp", "seq", None),
        ),
        out_specs=(
            P("dp", "seq", None),
            P("dp", "seq", None),
            P("dp", "seq", None),
            P("dp", "seq", None),
            P("dp", "seq", None),
            P("dp", "seq", None),
            P("seq", None),
            P("seq", None),
            P("seq", None),
            P("seq", None),
            P("seq", None),
            P("seq", None),
            P("seq"),
            P("seq", None),
            P("seq", None),
            P(None, "seq"),
            P(None, "seq"),
        ),
        check_vma=False,
    )
```

profile of v0, /device:TPU:0, one launch (start us, length us, event | category | flops | bytes accessed | tf_op | source)
XLA Modules:
  0.0 1261.0 jit_solution(12720225188353141975)
XLA Ops:
  13.8 13.5 %all_gather.33 = bf16[3,1024]{1,0:T(4,128)(2,1)S(1)} all-gather(bf16[3,128]{1,0:T(4,128)(2,1)S(1)} %copy-done.119), channel_id=1, replica_groups=mesh['dp'=4,'seq'=8] {'seq'}, dimensions={1}, use_global_device_ids=true | all-gather | bytes 6912 | tf_op jit(solution)/shard_map/all_gather | solution.py:121
  27.9 8.8 all_gather.34
  37.3 39.9 %all-gather.10.cloned.1.call-done = bf16[1024,3072]{1,0:T(8,128)(2,1)} async-done(((bf16[128,3072]{1,0:T(8,128)(2,1)}), bf16[1024,3072]{1,0:T(8,128)(2,1)}) %all-gather.10.cloned.1.call-update) | async-done | bytes 6291472 | tf_op jit(solution)/shard_map/all_gather | solution.py:112
  77.3 4.9 convolution_convert_fusion.3
  92.1 25.3 %all-gather = bf16[8,1,128]{2,1,0:T(2,128)(2,1)S(1)} all-gather(bf16[1,1,128]{2,1,0:T(2,128)(2,1)S(1)} %bitcast.493), channel_id=1, replica_groups=mesh['dp'=4,'seq'=8] {'seq'}, dimensions={0}, use_global_device_ids=true | all-gather | bytes 2304 | tf_op jit(solution)/shard_map/all_gather | solution.py:118
  120.6 3.9 copy.265
  124.5 6.6 all-to-all-start
  148.1 42.8 %all-to-all-done = bf16[2,80,3,1024]{1,0,2,3:T(2,128)(2,1)S(1)} async-done(((bf16[2,80,3,1024]{1,0,2,3:T(2,128)(2,1)}), bf16[2,80,3,1024]{1,0,2,3:T(2,128)(2,1)S(1)}, u32[]{:S(2)}, u32[]{:S(2)}) %all-to-all-start) | async-done | bytes 983072 | tf_op jit(solution)/shard_map/all_to_all | solution.py:178
  191.0 3.9 all-to-all-start.3
  197.8 6.4 fusion.187
  218.8 9.2 all-to-all-done.1
  231.3 25.1 %all-gather.18.cloned.1.call-done = bf16[1024,1024]{1,0:T(8,128)(2,1)} async-done(((bf16[128,1024]{1,0:T(8,128)(2,1)}), bf16[1024,1024]{1,0:T(8,128)(2,1)}) %all-gather.18.cloned.1.call-update) | async-done | bytes 2097168 | tf_op jit(solution)/shard_map/all_gather | solution.py:114
  269.0 11.6 all-to-all-done.6
  291.9 10.4 all-to-all-done.4
  309.5 11.2 all-to-all-done.7
  320.7 5.8 all-to-all-start.5
  326.8 20.5 %all-to-all-done.5 = bf16[2,640,128]{2,0,1:T(2,128)(2,1)S(1)} async-done(((bf16[2,640,128]{2,0,1:T(2,128)(2,1)}), bf16[2,640,128]{2,0,1:T(2,128)(2,1)S(1)}, u32[]{:S(2)}, u32[]{:S(2)}) %all-to-all-start.5) | async-done | bytes 327712 | tf_op jit(solution)/shard_map/all_to_all | solution.py:220
  352.0 40.1 %all-gather.22.cloned.1.call-done = bf16[1024,4096]{1,0:T(8,128)(2,1)} async-done(((bf16[128,4096]{1,0:T(8,128)(2,1)}), bf16[1024,4096]{1,0:T(8,128)(2,1)}) %all-gather.22.cloned.1.call-update) | async-done | bytes 8388624 | tf_op jit(solution)/shard_map/all_gather | solution.py:119
  392.1 17.1 %multiply_convert_fusion.1 = (bf16[288,4096]{1,0:T(8,128)(2,1)}, f32[288,4096]{1,0:T(8,128)}, f32[288,4096]{1,0:T(8,128)}) fusion(bf16[1024,4096]{1,0:T(8,128)(2,1)} %all-gather.22.cloned.1.call-done, f32[288,1024]{1,0:T(8,128)S(1)} %get-tuple-element.69, f32[1024]{0:T(1024)S(1)} %bitcast.487, f32[1024]{0:T(1024)S(1)} %bitcast.479, f32[288]{0:T(512)S(1)} %fusion.135, ...), kind=kOutput, calls=%fused_computation.15 | convolution fusion | flops 2494070784 | bytes 21375232 | tf_op jit(solution)/shard_map/dot_general | solution.py:31
  409.2 65.3 %all-gather.24.cloned.1.call-done = bf16[4096,1024]{1,0:T(8,128)(2,1)} async-done(((bf16[512,1024]{1,0:T(8,128)(2,1)}), bf16[4096,1024]{1,0:T(8,128)(2,1)}) %all-gather.24.cloned.1.call-update) | async-done | bytes 8388624 | tf_op jit(solution)/shard_map/all_gather | solution.py:120
  474.5 11.8 add_convert_fusion
  486.4 5.2 multiply_reduce_fusion.2
  502.8 7.6 all-to-all-done.10
  522.9 6.2 all-to-all-done.8
  541.7 12.5 reduce-scatter.39.cloned.1.call-done
  555.0 30.4 %reduce-scatter.37.cloned.1.call-done = bf16[8,2048]{1,0:T(8,128)(2,1)} async-done(((bf16[64,2048]{1,0:T(8,128)(2,1)}), bf16[8,2048]{1,0:T(8,128)(2,1)}) %reduce-scatter.37.cloned.1.call-update) | async-done | bytes 32784
  595.5 12.3 all-to-all-done.11
  611.5 15.8 %all-to-all-done.9 = bf16[2,640,128]{2,0,1:T(2,128)(2,1)S(1)} async-done(((bf16[2,640,128]{2,0,1:T(2,128)(2,1)}), bf16[2,640,128]{2,0,1:T(2,128)(2,1)S(1)}, u32[]{:S(2)}, u32[]{:S(2)}) %all-to-all-start.9) | async-done | bytes 327712 | tf_op jit(solution)/shard_map/all_to_all | solution.py:259
  652.1 7.8 all-to-all-done.14
  680.7 4.4 all-to-all-start.15
  685.9 4.1 multiply_reduce_fusion
  690.0 4.1 multiply_convert_fusion
  702.1 4.3 fusion.56
  709.6 6.0 all-to-all-done.15
  721.3 34.0 %all-to-all-done.13 = bf16[2,640,3,128]{3,0,2,1:T(2,128)(2,1)S(1)} async-done(((bf16[2,640,3,128]{3,0,2,1:T(2,128)(2,1)}), bf16[2,640,3,128]{3,0,2,1:T(2,128)(2,1)S(1)}, u32[]{:S(2)}, u32[]{:S(2)}) %all-to-all-start.13) | async-done | bytes 983072 | tf_op jit(solution)/shard_map/all_to_all | solution.py:333
  757.6 5.6 convolution_convert_fusion.2
  764.5 8.7 convolution_convert_fusion.1
  774.3 8.6 convolution_convert_fusion
  783.6 5.6 fusion.181
  792.1 25.8 %reduce-scatter.27.cloned.1.call-done = bf16[128,2048]{1,0:T(8,128)(2,1)} async-done(((bf16[1024,2048]{1,0:T(8,128)(2,1)}), bf16[128,2048]{1,0:T(8,128)(2,1)}) %reduce-scatter.27.cloned.1.call-update) | async-done | bytes 524304 | tf_op jit(solution)/shard_map/reduce_scatter | solution.py:365
  817.9 70.1 %reduce-scatter.21.cloned.1.call-done = bf16[128,3072]{1,0:T(8,128)(2,1)} async-done(((bf16[1024,3072]{1,0:T(8,128)(2,1)}), bf16[128,3072]{1,0:T(8,128)(2,1)}) %reduce-scatter.21.cloned.1.call-update) | async-done | bytes 786448 | tf_op jit(solution)/shard_map/reduce_scatter | solution.py:356
  888.0 90.2 %reduce-scatter.33.cloned.1.call-done = bf16[128,4096]{1,0:T(8,128)(2,1)} async-done(((bf16[1024,4096]{1,0:T(8,128)(2,1)}), bf16[128,4096]{1,0:T(8,128)(2,1)}) %reduce-scatter.33.cloned.1.call-update) | async-done | bytes 1048592 | tf_op jit(solution)/shard_map/reduce_scatter | solution.py:377
  978.2 90.1 %reduce-scatter.35.cloned.1.call-done = bf16[512,1024]{1,0:T(8,128)(2,1)} async-done(((bf16[4096,1024]{1,0:T(8,128)(2,1)}), bf16[512,1024]{1,0:T(8,128)(2,1)}) %reduce-scatter.35.cloned.1.call-update) | async-done | bytes 1048592 | tf_op jit(solution)/shard_map/reduce_scatter | solution.py:380
  1070.2 6.8 fusion.38
  1079.7 13.6 %all-reduce = bf16[1024]{0:T(1024)(128)(2,1)S(1)} all-reduce(bf16[1024]{0:T(1024)(128)(2,1)S(1)} %add_convert_fusion.3), channel_id=10, replica_groups=mesh['dp'=4,'seq'=8] {'seq'}, use_global_device_ids=true, to_apply=%region_40.41.clone | all-reduce | flops 1024 | bytes 4096
  1100.8 30.3 %reduce-scatter.41.cloned.1.call-done = bf16[128,3]{1,0:T(8,128)(2,1)} async-done(((bf16[1024,3]{1,0:T(8,128)(2,1)}), bf16[128,3]{1,0:T(8,128)(2,1)}) %reduce-scatter.41.cloned.1.call-update) | async-done | bytes 784
  1132.0 9.9 all-reduce.1
  1143.6 100.0 %all-reduce.5.cloned.1.call-done = (bf16[128,3072]{1,0:T(8,128)(2,1)}, bf16[128,1024]{1,0:T(8,128)(2,1)}, bf16[128,1024]{1,0:T(8,128)(2,1)}, bf16[128,2048]{1,0:...) async-done(((bf16[128,3072]{1,0:T(8,128)(2,1)}, bf16[128,1024]{1,0:T(8,128)(2,1)}, ...) | async-done | bytes 4390928 | tf_op jit(solution)/shard_map/psum | solution.py:387
  (543 shorter events, 239.0 us)
Async XLA Ops:
  7.2 209.7 %copy-start = (bf16[2,64,768]{2,1,0:T(8,128)(2,1)S(1)}, bf16[2,64,768]{2,1,0:T(8,128)(2,1)}, u32[]{:S(2)}) copy-start(bf16[2,64,768]{2,1,0:T(8,128)(2,1)} %param.22) | copy-start | bytes 589828
  7.2 70.0 %all-gather.10.cloned.1.call-start = ((), (), s32[]{:S(2)}) async-start(), calls=%async_computation.28 | async-start | bytes 7077888 | tf_op jit(solution)/shard_map/all_gather | solution.py:112
  8.0 207.0 %all-gather.14.cloned.1.call-start = ((), (), s32[]{:S(2)}) async-start(), calls=%async_computation.30 | async-start | bytes 1769472 | tf_op jit(solution)/shard_map/all_gather | solution.py:117
  8.7 208.6 %all-gather.16.cloned.1.call-start = ((), (), s32[]{:S(2)}) async-start(), calls=%async_computation.31 | async-start | bytes 4718592 | tf_op jit(solution)/shard_map/all_gather | solution.py:115
  9.5 218.8 %all-gather.12.cloned.1.call-start = ((), (), s32[]{:S(2)}) async-start(), calls=%async_computation.29 | async-start | bytes 2359296 | tf_op jit(solution)/shard_map/all_gather | solution.py:113
  10.0 246.4 %all-gather.18.cloned.1.call-start = ((), (), s32[]{:S(2)}) async-start(), calls=%async_computation.32 | async-start | bytes 2359296 | tf_op jit(solution)/shard_map/all_gather | solution.py:114
  10.6 338.3 %all-gather.20.cloned.1.call-start = ((), (), s32[]{:S(2)}) async-start(), calls=%async_computation.33 | async-start | bytes 2359296 | tf_op jit(solution)/shard_map/all_gather | solution.py:116
  11.2 380.8 %all-gather.22.cloned.1.call-start = ((), (), s32[]{:S(2)}) async-start(), calls=%async_computation.34 | async-start | bytes 9437184 | tf_op jit(solution)/shard_map/all_gather | solution.py:119
  12.0 462.6 %all-gather.24.cloned.1.call-start = ((), (), s32[]{:S(2)}) async-start(), calls=%async_computation.35 | async-start | bytes 9437184 | tf_op jit(solution)/shard_map/all_gather | solution.py:120
  12.9 64.4 %copy-start.88 = (f32[288]{0:T(512)}, f32[288]{0:T(512)S(1)}, u32[]{:S(2)}) copy-start(f32[288]{0:T(512)S(1)} %broadcast_multiply_fusion.2) | copy-start | bytes 3460
  13.8 63.4 %copy-start.92 = (f32[288]{0:T(512)}, f32[288]{0:T(512)S(1)}, u32[]{:S(2)}) copy-start(f32[288]{0:T(512)S(1)} %fusion.133) | copy-start | bytes 3460
  27.9 49.4 %copy-start.86 = (f32[1,1024]{1,0:T(1,128)}, f32[1,1024]{1,0:T(1,128)S(1)}, u32[]{:S(2)}) copy-start(f32[1,1024]{1,0:T(1,128)S(1)} %get-tuple-element.52) | copy-start | bytes 12292
  27.9 463.6 %copy-start.94 = (f32[1,1024]{1,0:T(1,128)}, f32[1,1024]{1,0:T(1,128)S(1)}, u32[]{:S(2)}) copy-start(f32[1,1024]{1,0:T(1,128)S(1)} %get-tuple-element.50) | copy-start | bytes 12292
  37.3 40.0 %copy-start.113 = (f32[1,1024]{1,0:T(1,128)}, f32[1,1024]{1,0:T(1,128)S(1)}, u32[]{:S(2)}) copy-start(f32[1,1024]{1,0:T(1,128)S(1)} %get-tuple-element.55) | copy-start | bytes 12292
  88.4 36.1 %all-to-all-start.2 = ((bf16[8,2,24576]{2,1,0:T(2,128)(2,1)}), bf16[8,2,24576]{2,1,0:T(2,128)(2,1)S(1)}, u32[]{:S(2)}, u32[]{:S(2)}) async-start(bf16[8,2,24576]{2,1,0:T(2,128)(2,1)} %reshape.558), calls=%async_computation.2 | async-start | bytes 1572864 | tf_op jit(solution)/shard_map/all_to_all | solution.py:179
  124.5 66.5 %all-to-all-start = ((bf16[2,80,3,1024]{1,0,2,3:T(2,128)(2,1)}), bf16[2,80,3,1024]{1,0,2,3:T(2,128)(2,1)S(1)}, u32[]{:S(2)}, u32[]{:S(2)}) async-start(bf16[2,80,3,1024]{1,0,2,3:T(2,128)(2,1)} %copy.265), calls=%async_computation | async-start | bytes 3145728 | tf_op jit(solution)/shard_map/all_to_all | solution.py:178
  191.0 20.5 %all-to-all-start.3 = ((bf16[2,512,128]{2,0,1:T(2,128)(2,1)}), bf16[2,512,128]{2,0,1:T(2,128)(2,1)S(1)}, u32[]{:S(2)}, u32[]{:S(2)}) async-start(bf16[2,512,128]{2,0,1:T(2,128)(2,1)} %copy.282), calls=%async_computation.3 | async-start | bytes 524288 | tf_op jit(solution)/shard_map/all_to_all | solution.py:187
  211.5 16.5 %all-to-all-start.1 = ((bf16[2,640,128]{2,0,1:T(2,128)(2,1)}), bf16[2,640,128]{2,0,1:T(2,128)(2,1)S(1)}, u32[]{:S(2)}, u32[]{:S(2)}) async-start(bf16[2,640,128]{2,0,1:T(2,128)(2,1)} %copy.272), calls=%async_computation.1 | async-start | bytes 655360 | tf_op jit(solution)/shard_map/all_to_all | solution.py:186
  261.2 19.4 %all-to-all-start.6 = ((bf16[8,2,8192]{2,1,0:T(2,128)(2,1)}), bf16[8,2,8192]{2,1,0:T(2,128)(2,1)S(1)}, u32[]{:S(2)}, u32[]{:S(2)}) async-start(bf16[8,2,8192]{2,1,0:T(2,128)(2,1)} %reshape.560), calls=%async_computation.6 | async-start | bytes 524288 | tf_op jit(solution)/shard_map/all_to_all | solution.py:195
  280.6 21.7 %all-to-all-start.4 = ((bf16[2,80,1024]{1,0,2:T(2,128)(2,1)}), bf16[2,80,1024]{1,0,2:T(2,128)(2,1)S(1)}, u32[]{:S(2)}, u32[]{:S(2)}) async-start(bf16[2,80,1024]{1,0,2:T(2,128)(2,1)} %copy.285), calls=%async_computation.4 | async-start | bytes 1048576 | tf_op jit(solution)/shard_map/all_to_all | solution.py:194
  302.3 18.4 %all-to-all-start.7 = ((bf16[2,512,128]{2,0,1:T(2,128)(2,1)}), bf16[2,512,128]{2,0,1:T(2,128)(2,1)S(1)}, u32[]{:S(2)}, u32[]{:S(2)}) async-start(bf16[2,512,128]{2,0,1:T(2,128)(2,1)} %copy.298), calls=%async_computation.7 | async-start | bytes 524288 | tf_op jit(solution)/shard_map/all_to_all | solution.py:221
  320.7 26.5 %all-to-all-start.5 = ((bf16[2,640,128]{2,0,1:T(2,128)(2,1)}), bf16[2,640,128]{2,0,1:T(2,128)(2,1)S(1)}, u32[]{:S(2)}, u32[]{:S(2)}) async-start(bf16[2,640,128]{2,0,1:T(2,128)(2,1)} %copy.290), calls=%async_computation.5 | async-start | bytes 655360 | tf_op jit(solution)/shard_map/all_to_all | solution.py:220
  348.9 43.1 %copy-start.111 = (f32[1,1024]{1,0:T(1,128)S(1)}, f32[1,1024]{1,0:T(1,128)}, u32[]{:S(2)}) copy-start(f32[1,1024]{1,0:T(1,128)} %get-tuple-element.53) | copy-start | bytes 12292
  351.7 139.9 %copy-start.4 = (f32[288,1024]{1,0:T(8,128)}, f32[288,1024]{1,0:T(8,128)S(1)}, u32[]{:S(2)}) copy-start(f32[288,1024]{1,0:T(8,128)S(1)} %get-tuple-element.69) | copy-start | bytes 3538948
  352.0 139.6 %copy-start.105 = (f32[288]{0:T(512)}, f32[288]{0:T(512)S(1)}, u32[]{:S(2)}) copy-start(f32[288]{0:T(512)S(1)} %fusion.135) | copy-start | bytes 3460
  392.0 82.5 %copy-start.23 = (bf16[2,80,1024]{2,1,0:T(8,128)(2,1)S(1)}, bf16[2,80,1024]{2,1,0:T(8,128)(2,1)}, u32[]{:S(2)}) copy-start(bf16[2,80,1024]{2,1,0:T(8,128)(2,1)} %param.38) | copy-start | bytes 983044
  497.3 13.1 %all-to-all-start.10 = ((bf16[8,2,8192]{2,1,0:T(2,128)(2,1)}), bf16[8,2,8192]{2,1,0:T(2,128)(2,1)S(1)}, u32[]{:S(2)}, u32[]{:S(2)}) async-start(bf16[8,2,8192]{2,1,0:T(2,128)(2,1)} %reshape.562), calls=%async_computation.10 | async-start | bytes 524288 | tf_op jit(solution)/shard_map/all_to_all | solution.py:243
  510.3 18.8 %all-to-all-start.8 = ((bf16[2,80,1024]{1,0,2:T(2,128)(2,1)}), bf16[2,80,1024]{1,0,2:T(2,128)(2,1)S(1)}, u32[]{:S(2)}, u32[]{:S(2)}) async-start(bf16[2,80,1024]{1,0,2:T(2,128)(2,1)} %copy.301), calls=%async_computation.8 | async-start | bytes 1048576 | tf_op jit(solution)/shard_map/all_to_all | solution.py:242
  513.8 40.4 %reduce-scatter.39.cloned.1.call-start = ((), (), s32[]{:S(2)}) async-start(), calls=%async_computation.45 | async-start | bytes 294912
  522.5 63.0 %reduce-scatter.37.cloned.1.call-start = ((), (), s32[]{:S(2)}) async-start(), calls=%async_computation.44 | async-start | bytes 294912
  537.9 254.1 %reduce-scatter.29.cloned.1.call-start = ((), (), s32[]{:S(2)}) async-start(), calls=%async_computation.40 | async-start | bytes 2359296 | tf_op jit(solution)/shard_map/reduce_scatter | solution.py:368
  541.7 250.4 %reduce-scatter.31.cloned.1.call-start = ((), (), s32[]{:S(2)}) async-start(), calls=%async_computation.41 | async-start | bytes 1769472 | tf_op jit(solution)/shard_map/reduce_scatter | solution.py:371
  590.6 17.1 %all-to-all-start.11 = ((bf16[2,512,128]{2,0,1:T(2,128)(2,1)}), bf16[2,512,128]{2,0,1:T(2,128)(2,1)S(1)}, u32[]{:S(2)}, u32[]{:S(2)}) async-start(bf16[2,512,128]{2,0,1:T(2,128)(2,1)} %copy.314), calls=%async_computation.11 | async-start | bytes 524288 | tf_op jit(solution)/shard_map/all_to_all | solution.py:260
  607.8 19.6 %all-to-all-start.9 = ((bf16[2,640,128]{2,0,1:T(2,128)(2,1)}), bf16[2,640,128]{2,0,1:T(2,128)(2,1)S(1)}, u32[]{:S(2)}, u32[]{:S(2)}) async-start(bf16[2,640,128]{2,0,1:T(2,128)(2,1)} %copy.306), calls=%async_computation.9 | async-start | bytes 655360 | tf_op jit(solution)/shard_map/all_to_all | solution.py:259
  611.2 180.9 %reduce-scatter.25.cloned.1.call-start = ((), (), s32[]{:S(2)}) async-start(), calls=%async_computation.38 | async-start | bytes 2359296 | tf_op jit(solution)/shard_map/reduce_scatter | solution.py:362
  630.3 161.8 %reduce-scatter.23.cloned.1.call-start = ((), (), s32[]{:S(2)}) async-start(), calls=%async_computation.37 | async-start | bytes 2359296 | tf_op jit(solution)/shard_map/reduce_scatter | solution.py:359
  642.6 17.4 %all-to-all-start.14 = ((bf16[8,2,8192]{2,1,0:T(2,128)(2,1)}), bf16[8,2,8192]{2,1,0:T(2,128)(2,1)S(1)}, u32[]{:S(2)}, u32[]{:S(2)}) async-start(bf16[8,2,8192]{2,1,0:T(2,128)(2,1)} %reshape.564), calls=%async_computation.14 | async-start | bytes 524288 | tf_op jit(solution)/shard_map/all_to_all | solution.py:316
  646.0 171.8 %reduce-scatter.27.cloned.1.call-start = ((), (), s32[]{:S(2)}) async-start(), calls=%async_computation.39 | async-start | bytes 4718592 | tf_op jit(solution)/shard_map/reduce_scatter | solution.py:365
  660.0 20.7 %all-to-all-start.12 = ((bf16[2,80,1024]{1,0,2:T(2,128)(2,1)}), bf16[2,80,1024]{1,0,2:T(2,128)(2,1)S(1)}, u32[]{:S(2)}, u32[]{:S(2)}) async-start(bf16[2,80,1024]{1,0,2:T(2,128)(2,1)} %copy.317), calls=%async_computation.12 | async-start | bytes 1048576 | tf_op jit(solution)/shard_map/all_to_all | solution.py:315
  680.7 34.9 %all-to-all-start.15 = ((bf16[2,512,3,128]{3,0,2,1:T(2,128)(2,1)}), bf16[2,512,3,128]{3,0,2,1:T(2,128)(2,1)}, u32[]{:S(2)}, u32[]{:S(2)}) async-start(bf16[2,512,3,128]{3,0,2,1:T(2,128)(2,1)} %pad_maximum_fusion.1), calls=%async_computation.15 | async-start | bytes 1572864 | tf_op jit(solution)/shard_map/all_to_all | solution.py:334
  715.6 39.7 %all-to-all-start.13 = ((bf16[2,640,3,128]{3,0,2,1:T(2,128)(2,1)}), bf16[2,640,3,128]{3,0,2,1:T(2,128)(2,1)S(1)}, u32[]{:S(2)}, u32[]{:S(2)}) async-start(bf16[2,640,3,128]{3,0,2,1:T(2,128)(2,1)} %pad_maximum_fusion), calls=%async_computation.13 | async-start | bytes 1966080 | tf_op jit(solution)/shard_map/all_to_all | solution.py:333
  719.2 168.9 %reduce-scatter.21.cloned.1.call-start = ((), (), s32[]{:S(2)}) async-start(), calls=%async_computation.36 | async-start | bytes 7077888 | tf_op jit(solution)/shard_map/reduce_scatter | solution.py:356
  763.2 214.9 %reduce-scatter.33.cloned.1.call-start = ((), (), s32[]{:S(2)}) async-start(), calls=%async_computation.42 | async-start | bytes 9437184 | tf_op jit(solution)/shard_map/reduce_scatter | solution.py:377
  773.2 295.1 %reduce-scatter.35.cloned.1.call-start = ((), (), s32[]{:S(2)}) async-start(), calls=%async_computation.43 | async-start | bytes 9437184 | tf_op jit(solution)/shard_map/reduce_scatter | solution.py:380
  782.9 317.1 %reduce-scatter.43.cloned.1.call-start = ((), (), s32[]{:S(2)}) async-start(), calls=%async_computation.47 | async-start | bytes 294912
  789.2 279.1 %copy-start.13 = (f32[288,1024]{1,0:T(8,128)}, f32[288,1024]{1,0:T(8,128)S(1)}, u32[]{:S(2)}) copy-start(f32[288,1024]{1,0:T(8,128)S(1)} %get-tuple-element.81) | copy-start | bytes 3538948
  791.0 340.2 %reduce-scatter.41.cloned.1.call-start = ((), (), s32[]{:S(2)}) async-start(), calls=%async_computation.46 | async-start | bytes 294912
  792.0 451.6 %all-reduce.5.cloned.1.call-start = ((), (), s32[]{:S(2)}) async-start(), calls=%async_computation.48 | async-start | bytes 8781824 | tf_op jit(solution)/shard_map/psum | solution.py:387
  (121 other events, 848.5 us)
Sparse Core Ops, SparseCore 0:
  9.7 67.5 all-gather.9
  78.9 29.3 all-gather.13
  109.9 76.7 all-gather.15
  188.1 39.4 all-gather.11
  229.1 27.2 all-gather.17
  257.9 38.9 all-gather.19
  298.4 93.5 all-gather.21
  393.6 80.8 all-gather.23
  522.6 31.6 reduce-scatter.38
  557.0 28.4 reduce-scatter.36
  587.8 39.4 reduce-scatter.28
  630.0 37.3 reduce-scatter.30
  670.3 40.5 reduce-scatter.24
  713.6 51.3 reduce-scatter.22
  767.2 50.6 reduce-scatter.26
  820.0 67.9 reduce-scatter.20
  890.2 87.9 reduce-scatter.32
  980.3 87.9 reduce-scatter.34
  1071.1 28.8 reduce-scatter.42
  1102.8 28.3 reduce-scatter.40
  1135.7 107.7 all-reduce.4
where the time goes:
time: 1270 us; the launch traced here: 1260 us
  waiting for transfers between devices  830 us (65%)
  matrix products  165 us (13%)
  local copies, waits for them, and re-layouts  80.6 us (6%)
  blocking collectives  71.1 us (6%)
  starting transfers between devices  64.3 us (5%)
  other arithmetic  32.7 us (3%)
  between operations  17.7 us (1%)
    psum x1, waiting for transfers between devices, on_device(): lax.psum(shares[0].astype(jnp.bfloat16), 'dp').astype(jnp.float32)  100 us
    reduce_scatter x1, waiting for transfers between devices, on_device(): lax.psum_scatter(grads[7].astype(jnp.bfloat16), 'seq', scatter_dimension=...  90.2 us
    reduce_scatter x1, waiting for transfers between devices, on_device(): lax.psum_scatter(grads[8].astype(jnp.bfloat16), 'seq', scatter_dimension=...  90.1 us
    unnamed x25, waiting for transfers between devices  81.7 us
    reduce_scatter x1, waiting for transfers between devices, on_device(): lax.psum_scatter(grads[0].astype(jnp.bfloat16), 'seq', scatter_dimension=...  70.1 us
    all_gather x1, waiting for transfers between devices, on_device(): lax.all_gather(feed_out, 'seq', axis=0, tiled=True)  65.3 us
    dot_general x12, matrix products, product(): return jnp.dot(left, right, preferred_element_type=jnp.float32)  43.7 us
    all_to_all x1, waiting for transfers between devices, self_heads(): lax.all_to_all(long_part, 'seq', split_axis=3, concat_axis=1, tiled=True)  42.8 us
  transfers between devices with their start and end apart: 37, of which 28 were waited for; matrix products, arithmetic and copies ran while one was open for 19% of the time, Pallas kernels for 0%

commit v1 on v0

--- a/solution.py
+++ b/solution.py
@@ -3,6 +3,8 @@
 import jax
 import jax.numpy as jnp
 from jax import lax
+from jax.experimental import pallas as pl
+from jax.experimental.pallas import tpu as pltpu
 from jax.sharding import PartitionSpec as P
 
 D = 1024
@@ -419,9 +421,817 @@
     )
 
 
+STAGES = 4
+PARTS = 4
+ALL_AXES = ("dp", "seq")
+
+
+def fits_item_plan(mesh):
+    return dict(mesh.shape) == {"dp": PARTS, "seq": 2 * STAGES}
+
+
+def partner(values):
+    return lax.ppermute(values, "seq", [(rank, rank ^ 1) for rank in range(2 * STAGES)])
+
+
+def next_stage(values):
+    count = 2 * STAGES
+    return lax.ppermute(values, "seq", [(rank, (rank + 2) % count) for rank in range(count)])
+
+
+def across(values, second):
+    pairs = []
+    for group in range(PARTS):
+        for rank in range(2 * STAGES):
+            flip = 1 + rank % 2 if not second else 2 - rank % 2
+            pairs.append((group * 2 * STAGES + rank, (group ^ flip) * 2 * STAGES + rank))
+    return lax.ppermute(values, ALL_AXES, pairs)
+
+
+def stage_exchange(blocks):
+    groups = [[2 * stage + core for stage in range(STAGES)] for core in range(2)]
+    return lax.all_to_all(
+        blocks, "seq", split_axis=0, concat_axis=0, axis_index_groups=groups, tiled=True
+    )
+
+
+def part_of(group, core, slot):
+    flips = (0, 1 + core, 2 - core, 3)
+    return lax.bitwise_xor(group, flips[slot])
+
+
+def kernel_params(limit=40 << 20):
+    return pltpu.CompilerParams(vmem_limit_bytes=limit)
+
+
+VMEM_SPEC = pl.BlockSpec(memory_space=pltpu.VMEM)
+SMEM_SPEC = pl.BlockSpec(memory_space=pltpu.SMEM)
+ANY_SPEC = pl.BlockSpec(memory_space=pl.ANY)
+
+
+LANES = 512
+
+
+def after(values, *others):
+    return lax.optimization_barrier((values, *others))[0]
+
+
+def run_moves(moves, sems):
+    started = []
+    for number, (source, target) in enumerate(moves):
+        move = pltpu.make_async_copy(source, target, sems.at[number])
+        move.start()
+        started.append(move)
+    for move in started:
+        move.wait()
+
+
+def move_call(place, operands, out_shapes, plan):
+    n, m = len(operands), len(out_shapes)
+
+    class Blank:
+        @property
+        def at(self):
+            return self
+
+        def __getitem__(self, _):
+            return self
+
+    count = len(plan((0, 0, 0), [Blank()] * n, [Blank()] * m))
+
+    def kernel(place_ref, *refs):
+        spots = (place_ref[0], place_ref[1], place_ref[2])
+        run_moves(plan(spots, refs[:n], refs[n : n + m]), refs[n + m])
+
+    return pl.pallas_call(
+        kernel,
+        out_shape=[jax.ShapeDtypeStruct(shape, jnp.bfloat16) for shape in out_shapes],
+        in_specs=[SMEM_SPEC] + [ANY_SPEC] * n,
+        out_specs=[ANY_SPEC] * m,
+        scratch_shapes=[pltpu.SemaphoreType.DMA((count,))],
+        compiler_params=kernel_params(16 << 20),
+    )(place, *operands)
+
+
+def aligned(value, unit):
+    return value if isinstance(value, int) else pl.multiple_of(value, unit)
+
+
+class Split:
+    def __init__(self, matrix, width, halves=False):
+        self.matrix, self.width, self.halves = matrix, width, halves
+        self.rows = matrix.shape[0]
+        self.count = matrix.shape[1] // 2 // LANES
+        self.part_rows = self.rows * 2 // PARTS
+        self.shape = (self.rows * 2 * STAGES, matrix.shape[1] // 2)
+
+
+class Whole:
+    def __init__(self, matrix):
+        self.matrix = matrix
+        self.rows = matrix.shape[0]
+        self.count = matrix.shape[1] // LANES
+        self.part_rows = self.rows // PARTS
+        self.shape = (self.rows * STAGES, matrix.shape[1])
+
+
+def cut_columns(place, splits):
+    total = 0
+    for entry in splits:
+        entry.start = total
+        total += entry.rows * entry.count
+
+    def plan(spots, refs, outs):
+        moves = []
+        for ref, entry in zip(refs, splits):
+            width = entry.width
+            for j in range(entry.count * LANES // width):
+                target = (
+                    pl.ds(entry.start + j * width // LANES * entry.rows, entry.rows),
+                    pl.ds(j * width % LANES, width),
+                )
+                for side, out in enumerate(outs):
+                    core = spots[2] if side == 0 else 1 - spots[2]
+                    column = core * LANES if entry.halves else (2 * j + core) * width
+                    moves.append((ref.at[:, pl.ds(aligned(column, 128), width)], out.at[target]))
+        return moves
+
+    mine, others = move_call(
+        place, [entry.matrix for entry in splits], [(total, LANES)] * 2, plan
+    )
+    return mine, partner(others)
+
+
+def pack_parts(place, entries, packed):
+    wholes = [entry for entry in entries if isinstance(entry, Whole)]
+    total = 0
+    for entry in entries:
+        entry.offset = total
+        total += entry.part_rows * entry.count
+    operands = list(packed or ()) + [entry.matrix for entry in wholes]
+    first = len(operands) - len(wholes)
+
+    def sources(spots, refs, flipped):
+        moves = []
+        for entry in entries:
+            size = entry.part_rows
+            for j in range(entry.count):
+                if isinstance(entry, Whole):
+                    ref = refs[first + wholes.index(entry)]
+                    row = aligned(spots[1] * size, size)
+                    source = ref.at[pl.ds(row, size), pl.ds(j * LANES, LANES)]
+                else:
+                    row = entry.start + j * entry.rows + (spots[1] & 1) * size
+                    source = refs[1 if flipped else 0].at[pl.ds(aligned(row, 16), size)]
+                moves.append((source, (pl.ds(entry.offset + j * size, size),)))
+        return moves
+
+    n = len(operands)
+    count = sum(entry.count for entry in entries)
+
+    def kernel(place_ref, *refs):
+        spots = (place_ref[0], place_ref[1], place_ref[2])
+        out, sems = refs[n], refs[n + 1]
+        other = lax.bitwise_xor(lax.shift_right_logical(spots[1], 1), spots[2])
+        for flipped in range(2):
+
+            @pl.when(other == flipped)
+            def _():
+                moves = sources(spots, refs, flipped == 1)
+                run_moves([(source, out.at[target]) for source, target in moves], sems)
+
+    return pl.pallas_call(
+        kernel,
+        out_shape=jax.ShapeDtypeStruct((total, LANES), jnp.bfloat16),
+        in_specs=[SMEM_SPEC] + [ANY_SPEC] * n,
+        out_specs=ANY_SPEC,
+        scratch_shapes=[pltpu.SemaphoreType.DMA((count,))],
+        compiler_params=kernel_params(16 << 20),
+    )(place, *operands)
+
+
+def stage_hops(mine):
+    hops = []
+    for _ in range(STAGES - 1):
+        mine = next_stage(mine)
+        hops.append(mine)
+    return hops
+
+
+def share_hops(hops):
+    stack = jnp.stack(hops)
+    first = across(stack, False)
+    second = across(stack, True)
+    return stack, first, second, across(first, True)
+
+
+def assemble(place, entries, packed, shared):
+    wholes = [entry for entry in entries if isinstance(entry, Whole)]
+    operands = list(shared) + list(packed or ()) + [entry.matrix for entry in wholes]
+    first = len(operands) - len(wholes)
+
+    def plan(spots, refs, outs):
+        stage, group, core = spots
+        moves = []
+        for out, entry in zip(outs, entries):
+            size = entry.part_rows
+            rows = size * PARTS
+            for j in range(entry.count):
+                lanes = pl.ds(j * LANES, LANES)
+                if isinstance(entry, Whole):
+                    moves.append(
+                        (
+                            refs[first + wholes.index(entry)].at[:, lanes],
+                            out.at[pl.ds(aligned(stage * rows, rows), rows), lanes],
+                        )
+                    )
+                else:
+                    for side in range(2):
+                        row = stage * rows + (core if side == 0 else 1 - core) * entry.rows
+                        moves.append(
+                            (
+                                refs[4 + side].at[
+                                    pl.ds(entry.start + j * entry.rows, entry.rows)
+                                ],
+                                out.at[pl.ds(aligned(row, entry.rows), entry.rows), lanes],
+                            )
+                        )
+                for hop in range(1, STAGES):
+                    source_stage = (stage + STAGES - hop) & (STAGES - 1)
+                    for slot in range(PARTS):
+                        part = group ^ (0, 1 + core, 2 - core, 3)[slot]
+                        row = aligned(source_stage * rows + part * size, size)
+                        moves.append(
+                            (
+                                refs[slot].at[hop - 1, pl.ds(entry.offset + j * size, size)],
+                                out.at[pl.ds(row, size), lanes],
+                            )
+                        )
+        return moves
+
+    return move_call(place, operands, [entry.shape for entry in entries], plan)
+
+
+def group_blocks(place, pairs, shape, sums=None):
+    n = len(pairs)
+
+    def kernel(place_ref, *refs):
+        stage, group, core = place_ref[0], place_ref[1], place_ref[2]
+        far_ref, near_ref = refs[-2:]
+        for to_stage in range(STAGES):
+            hop = (stage + STAGES - to_stage) & (STAGES - 1)
+            results = []
+            for number, (left, right, _) in enumerate(pairs):
+                rows = left.shape[1] // STAGES
+                results.append(
+                    lax.dot_general(
+                        refs[2 * number][:, to_stage * rows : (to_stage + 1) * rows],
+                        refs[2 * number + 1][...],
+                        (((0,), (0,)), ((), ())),
+                        preferred_element_type=jnp.float32,
+                    ).astype(jnp.bfloat16)
+                )
+            for part in range(PARTS):
+                apart = group ^ part
+                slot = jnp.where((core == 1) & (apart != 0) & (apart != 3), 3 - apart, apart)
+                slot = jnp.asarray(slot, jnp.int32)
+
+                def put(out_ref, index):
+                    for result, (left, right, moves) in zip(results, pairs):
+                        columns = right.shape[1] // PARTS
+                        for first, count, row, lane in moves:
+                            out_ref[index, hop, row : row + count, lane : lane + columns] = result[
+                                first : first + count, part * columns : (part + 1) * columns
+                            ]
+                    if sums is not None:
+                        for side in range(2):
+                            row = shape[0] // 2 * (side + 1) - 16
+                            lane = 256 * to_stage + 128 * side
+                            out_ref[index, hop, row : row + 16, 0:128] = refs[2 * n][
+                                part, :, lane : lane + 128
+                            ]
+                            out_ref[index, hop, row : row + 16, 128:] = jnp.zeros(
+                                (16, shape[1] - 128), jnp.bfloat16
+                            )
+
+                @pl.when(slot >= 2)
+                def _():
+                    put(far_ref, slot - 2)
+
+                @pl.when(slot < 2)
+                def _():
+                    put(near_ref, slot)
+
+    operands = [array for left, right, _ in pairs for array in (left, right)]
+    if sums is not None:
+        operands.append(sums)
+    return pl.pallas_call(
+        kernel,
+        out_shape=[jax.ShapeDtypeStruct((2, STAGES, *shape), jnp.bfloat16)] * 2,
+        in_specs=[SMEM_SPEC] + [VMEM_SPEC] * len(operands),
+        out_specs=[VMEM_SPEC] * 2,
+        compiler_params=kernel_params(48 << 20),
+    )(place, *operands)
+
+
+def wide(values):
+    return values.astype(jnp.float32)
+
+
+def narrow(values):
+    return values.astype(jnp.bfloat16)
+
+
+def reduce_group(far, near):
+    got = across(far, True)
+    send = narrow(wide(near[1]) + wide(got[1]))
+    kept = wide(near[0]) + wide(got[0])
+    other = across(send, False)
+    total = kept + wide(other)
+    moving = next_stage(narrow(total[1]))
+    moving = next_stage(narrow(total[2] + wide(moving)))
+    moving = next_stage(narrow(total[3] + wide(moving)))
+    return narrow(total[0] + wide(moving))
+
+
+def finish(place, block, outs, sums=False):
+    first = across(block, False)
+    second = across(block, True)
+    third = across(first, True)
+
+    def kernel(place_ref, *refs):
+        for slot in range(PARTS):
+            part = part_of(place_ref[1], place_ref[2], slot)
+            held = refs[slot]
+            for out_ref, (_, moves) in zip(refs[PARTS:], outs):
+                for index, size, start in moves:
+                    column = pl.multiple_of(start(part), 128)
+                    out_ref[:, pl.ds(column, size)] = held[index].astype(jnp.float32)
+            if sums:
+                tail = held[:, block.shape[1] - 16 :, 0:128].astype(jnp.float32)
+                refs[-1][part] = tail[0] + tail[1]
+
+    shapes = [shape for shape, _ in outs] + ([(PARTS, 16, 128)] if sums else [])
+    return pl.pallas_call(
+        kernel,
+        out_shape=[jax.ShapeDtypeStruct(shape, jnp.float32) for shape in shapes],
+        in_specs=[SMEM_SPEC] + [VMEM_SPEC] * PARTS,
+        out_specs=[VMEM_SPEC] * len(shapes),
+        compiler_params=kernel_params(),
+    )(place, block, first, second, third)
+
+
+def kept_scores(query, keys, valid, first_row, causal):
+    scores = (
+        lax.dot_general(
+            query, keys, (((1,), (1,)), ((), ())), preferred_element_type=jnp.float32
+        )
+        * 0.125
+    )
+    keep = valid > 0
+    if causal:
+        rows = first_row + lax.broadcasted_iota(jnp.int32, scores.shape, 0)
+        keep = keep & (lax.broadcasted_iota(jnp.int32, scores.shape, 1) <= rows)
+    return jnp.where(keep, scores, masked_value)
+
+
+def probabilities(scores):
+    raised = jnp.exp(scores - jnp.max(scores, -1, keepdims=True))
+    return raised / jnp.sum(raised, -1, keepdims=True)
+
+
+def chunks_of(length, causal):
+    if not causal:
+        return [(0, length, None)]
+    return [(start, 128, start + 128) for start in range(0, length, 128)]
+
+
+def attend_kernel(causal, valid_ref, q_ref, k_ref, v_ref, out_ref):
+    keys_count = k_ref.shape[0]
+    for head in range(2):
+        lanes = slice(64 * head, 64 * head + 64)
+        for start, size, limit in chunks_of(q_ref.shape[0], causal):
+            limit = limit or keys_count
+            scores = kept_scores(
+                q_ref[start : start + size, lanes],
+                k_ref[:limit, lanes],
+                valid_ref[:, :limit],
+                start,
+                causal,
+            )
+            weights = narrow(probabilities(scores))
+            out_ref[start : start + size, lanes] = narrow(product(weights, v_ref[:limit, lanes]))
+
+
+def attend_pair(valid, query, keys, values, causal):
+    length, count = query[0].shape[0], keys[0].shape[0]
+    return pl.pallas_call(
+        partial(attend_kernel, causal),
+        out_shape=jax.ShapeDtypeStruct((length, 512), jnp.bfloat16),
+        grid=(4,),
+        in_specs=[pl.BlockSpec((1, count), lambda pair: (0, 0))]
+        + [
+            pl.BlockSpec((size, 128), lambda pair, first=first: (0, first + pair))
+            for size, first in (
+                (length, query[1]),
+                (count, keys[1]),
+                (count, values[1]),
+            )
+        ],
+        out_specs=pl.BlockSpec((length, 128), lambda pair: (0, pair)),
+        compiler_params=kernel_params(),
+    )(valid, query[0], keys[0], values[0])
+
+
+def attend_back_kernel(causal, valid_ref, q_ref, k_ref, v_ref, do_ref, dq_ref, dk_ref, dv_ref, key_sum, value_sum):
+    keys_count = k_ref.shape[0]
+    for head in range(2):
+        lanes = slice(64 * head, 64 * head + 64)
+        key_sum[...] = jnp.zeros_like(key_sum)
+        value_sum[...] = jnp.zeros_like(value_sum)
+        for start, size, limit in chunks_of(q_ref.shape[0], causal):
+            limit = limit or keys_count
+            query = q_ref[start : start + size, lanes]
+            keys = k_ref[:limit, lanes]
+            grad_out = do_ref[start : start + size, lanes]
+            scores = kept_scores(query, keys, valid_ref[:, :limit], start, causal)
+            probs = probabilities(scores)
+            grad_probs = product_t(grad_out, v_ref[:limit, lanes])
+            centre = jnp.sum(probs * grad_probs, -1, keepdims=True)
+            grad_scores = narrow(probs * (grad_probs - centre))
+            value_sum[:limit] += weight_grad(narrow(probs), grad_out)
+            key_sum[:limit] += weight_grad(grad_scores, query)
+            dq_ref[start : start + size, lanes] = narrow(product(grad_scores, keys) * 0.125)
+        dk_ref[:, lanes] = narrow(key_sum[...] * 0.125)
+        dv_ref[:, lanes] = narrow(value_sum[...])
+
+
+def attend_back_pair(valid, query, keys, values, grad_out, causal):
+    length, count = query[0].shape[0], keys[0].shape[0]
+    return pl.pallas_call(
+        partial(attend_back_kernel, causal),
+        out_shape=[
+            jax.ShapeDtypeStruct((size, 512), jnp.bfloat16) for size in (length, count, count)
+        ],
+        grid=(4,),
+        in_specs=[pl.BlockSpec((1, count), lambda pair: (0, 0))]
+        + [
+            pl.BlockSpec((size, 128), lambda pair, first=first: (0, first + pair))
+            for size, first in (
+                (length, query[1]),
+                (count, keys[1]),
+                (count, values[1]),
+                (length, 0),
+            )
+        ],
+        out_specs=[
+            pl.BlockSpec((size, 128), lambda pair: (0, pair)) for size in (length, count, count)
+        ],
+        scratch_shapes=[pltpu.VMEM((count, 64), jnp.float32)] * 2,
+        compiler_params=kernel_params(),
+    )(valid, query[0], keys[0], values[0], grad_out)
+
+
+def normalise(values):
+    centred = values - jnp.mean(values, -1, keepdims=True)
+    scale = lax.rsqrt(jnp.mean(centred * centred, -1, keepdims=True) + norm_eps)
+    return centred * scale, scale
+
+
+def normal_back(unit, scale, gain_row, incoming):
+    scaled = incoming * gain_row
+    mean_one = jnp.mean(scaled, -1, keepdims=True)
+    mean_two = jnp.mean(scaled * unit, -1, keepdims=True)
+    return scale * (scaled - mean_one - unit * mean_two)
+
+
+def on_item_device(
+    long_frames,
+    short_frames,
+    long_text,
+    short_text,
+    long_lengths,
+    short_lengths,
+    text_lengths,
+    qkv_weight,
+    self_out,
+    cross_query,
+    cross_keyval,
+    cross_out,
+    text_proj,
+    text_bias,
+    feed_in,
+    feed_out,
+    norm_gains,
+    norm_shifts,
+    long_cot,
+    short_cot,
+):
+    rank, group = lax.axis_index("seq"), lax.axis_index("dp")
+    stage, core = rank // 2, rank % 2
+    place = jnp.stack([stage, group, core]).astype(jnp.int32)
+    is_first = core == 0
+    rows, short_rows = long_frames.shape[1], short_frames.shape[1]
+    length = rows * 2 * STAGES
+    text_count = long_text.shape[1]
+
+    def by_core(mine, other):
+        return jnp.where(is_first, mine, other), jnp.where(is_first, other, mine)
+
+    def blocks_of(long_part, short_part):
+        padded = jnp.pad(short_part, ((0, 0), (0, rows - short_rows), (0, 0)))
+        return jnp.concatenate([long_part, padded], 0)
+
+    half = D // 2
+    qkv_entry = [Split(qkv_weight, 128)]
+    qkv_packed = cut_columns(place, qkv_entry)
+    qkv_hops = stage_hops(pack_parts(place, qkv_entry, qkv_packed))
+
+    params = jnp.concatenate([norm_gains, norm_shifts, text_bias[None]], 0)
+    params = jnp.pad(params, ((0, 9), (0, D - params.shape[1])))
+    frames = jnp.concatenate(
+        [blocks_of(long_frames, short_frames), jnp.broadcast_to(params, (STAGES, 16, D))], 1
+    )
+    frames = stage_exchange(after(frames, qkv_packed[1]))
+    frames = jnp.stack(by_core(frames, partner(frames)), 1)
+    inputs = wide(frames[:, :, :rows].reshape(length, D))
+    small = wide(frames[:, :, rows : rows + 7, : D // 8].transpose(2, 0, 1, 3).reshape(7, D))
+    gains, shifts, bias = small[0:3], small[3:6], small[6]
+
+    splits = [
+        Split(after(cross_query, qkv_packed[1]), 128),
+        Split(cross_keyval, 128),
+        Split(text_proj, LANES, True),
+        Split(feed_in, 512),
+    ]
+    packed = cut_columns(place, splits)
+    (w_qkv,) = assemble(place, qkv_entry, qkv_packed, share_hops(qkv_hops))
+
+    middle_entry = [Whole(self_out), *splits[:3], Whole(cross_out)]
+    mine = pack_parts(place, middle_entry, packed)
+    middle_hops = stage_hops(after(mine, qkv_hops[1]))
+    w_self, w_query, w_keyval, w_text, w_cross = assemble(
+        place, middle_entry, packed, share_hops(middle_hops)
+    )
+    in_entry = [splits[3]]
+    in_hops = stage_hops(after(pack_parts(place, in_entry, packed), middle_hops[1]))
+    (w_in,) = assemble(place, in_entry, packed, share_hops(in_hops))
+    out_entry = [Whole(feed_out)]
+    out_hops = stage_hops(after(pack_parts(place, out_entry, None), in_hops[1]))
+    (w_out,) = assemble(place, out_entry, None, share_hops(out_hops))
+
+    cots = stage_exchange(after(blocks_of(long_cot, short_cot), out_hops[0]))
+    cots = jnp.stack(by_core(cots, partner(cots)), 1).reshape(length, D)
+
+    spots = jnp.arange(length)
+    real_rows = jnp.where(stage < STAGES // 2, rows, short_rows)
+    frame_limit = lax.dynamic_index_in_dim(
+        jnp.concatenate([long_lengths, short_lengths]), stage, keepdims=False
+    )
+    inside = spots % rows < real_rows
+    valid = inside & ((spots // rows) * real_rows + spots % rows < frame_limit)
+    valid = valid.astype(jnp.float32)[None]
+    text_limit = lax.dynamic_index_in_dim(
+        jnp.concatenate([text_lengths[0], text_lengths[1]]), stage, keepdims=False
+    )
+    text_valid = (jnp.arange(text_count) < text_limit).astype(jnp.float32)[None]
+    words = lax.dynamic_index_in_dim(
+        jnp.concatenate([long_text, short_text], 0), stage, keepdims=False
+    )
+
+    def pair_sum(part):
+        return part + wide(partner(narrow(part)))
+
+    unit0, scale0 = normalise(inputs)
+    normed0 = narrow(unit0 * gains[0] + shifts[0])
+    qkv = narrow(product(normed0, w_qkv))
+    mixed = attend_pair(valid, (qkv, 0), (qkv, 4), (qkv, 8), True)
+    after_self = inputs + pair_sum(product(mixed, w_self))
+    unit1, scale1 = normalise(after_self)
+    normed1 = narrow(unit1 * gains[1] + shifts[1])
+    query = narrow(product(normed1, w_query))
+    bias_mine = lax.dynamic_slice_in_dim(bias, core * half, half)
+    encoded = narrow(product(words, w_text) + bias_mine)
+    encoded = jnp.concatenate(by_core(encoded, partner(encoded)), 1)
+    keyval = narrow(product(encoded, w_keyval))
+    cross = attend_pair(text_valid, (query, 0), (keyval, 0), (keyval, 4), False)
+    after_cross = after_self + pair_sum(product(cross, w_cross))
+    unit2, scale2 = normalise(after_cross)
+    normed2 = narrow(unit2 * gains[2] + shifts[2])
+    pre_act = product(normed2, w_in)
+    hidden = narrow(jax.nn.gelu(pre_act, approximate=False))
+
+    def split_rows(values):
+        parts = values.reshape(STAGES, 2, rows, D)
+        mine = lax.dynamic_index_in_dim(parts, core, 1, keepdims=False)
+        other = lax.dynamic_index_in_dim(parts, 1 - core, 1, keepdims=False)
+        return mine, other
+
+    def back_to_frames(values):
+        moved = stage_exchange(narrow(values))
+        return moved[: STAGES // 2], moved[STAGES // 2 :, :short_rows]
+
+    out_mine, out_other = split_rows(product(hidden, w_out))
+    base_mine, _ = split_rows(after_cross)
+    long_output, short_output = back_to_frames(
+        base_mine + out_mine + wide(partner(narrow(out_other)))
+    )
+
+    def own_rows(block):
+        cut = block.reshape(2, block.shape[0] // 2, block.shape[1])
+        mine = lax.dynamic_index_in_dim(cut, core, 0, keepdims=False)
+        other = lax.dynamic_index_in_dim(cut, 1 - core, 0, keepdims=False)
+        return jnp.stack(by_core(mine, partner(other)))
+
+    hidden_rows = feed_out.shape[0]
+    feed_out_block = reduce_group(
+        *group_blocks(place, [(hidden, cots, [(0, hidden_rows, 0, 0)])], (hidden_rows, 256))
+    )
+    _, gelu_pull = jax.vjp(partial(jax.nn.gelu, approximate=False), pre_act)
+    grad_pre = narrow(gelu_pull(product_t(cots, w_out))[0])
+    feed_in_block = reduce_group(
+        *group_blocks(place, [(normed2, grad_pre, [(0, 256, 0, 0)])], (256, 512))
+    )
+    part2 = product_t(grad_pre, w_in)
+    grad_norm2 = pair_sum(part2)
+    grad_after_cross = wide(cots) + normal_back(unit2, scale2, gains[2], grad_norm2)
+    branch2 = narrow(grad_after_cross)
+    grad_cross = narrow(product_t(branch2, w_cross))
+    grad_query, grad_key, grad_value = attend_back_pair(
+        text_valid, (query, 0), (keyval, 0), (keyval, 4), grad_cross, False
+    )
+    part1 = product_t(grad_query, w_query)
+    grad_norm1 = pair_sum(part1)
+    grad_after_self = grad_after_cross + normal_back(unit1, scale1, gains[1], grad_norm1)
+    grad_keyval = jnp.concatenate([grad_key, grad_value], 1)
+    grad_encoded = narrow(pair_sum(product_t(grad_keyval, w_keyval)))
+    grad_encoded_mine = lax.dynamic_slice_in_dim(grad_encoded, core * half, half, 1)
+    text_rows = ENC // (2 * STAGES)
+    words_padded = jnp.pad(
+        words.reshape(text_count, 2 * STAGES, text_rows), ((0, 0), (0, 0), (0, 128 - text_rows))
+    ).reshape(text_count, D)
+    grad_words = product_t(grad_encoded_mine, w_text).reshape(STAGES, 2, -1, ENC)
+    words_mine = lax.dynamic_index_in_dim(grad_words, core, 1, keepdims=False)
+    words_other = lax.dynamic_index_in_dim(grad_words, 1 - core, 1, keepdims=False)
+    moved = wide(stage_exchange(narrow(words_mine + wide(partner(narrow(words_other))))))
+    long_text_grad, short_text_grad = moved[: STAGES // 2], moved[STAGES // 2 :]
+
+    branch1 = narrow(grad_after_self)
+    middle_block = reduce_group(
+        *group_blocks(
+            place,
+            [
+                (cross, branch2, [(0, 128, 0, 0)]),
+                (mixed, branch1, [(0, 128, 128, 0)]),
+                (normed1, grad_query, [(0, 256, 256, 0)]),
+                (words_padded, grad_encoded_mine, [(0, 256, 256, 128)]),
+                (encoded, grad_keyval, [(0, 256, 512, 0)]),
+            ],
+            (768, 256),
+        )
+    )
+    grad_mixed = narrow(product_t(branch1, w_self))
+    grad_qkv = jnp.concatenate(
+        attend_back_pair(valid, (qkv, 0), (qkv, 4), (qkv, 8), grad_mixed, True), 1
+    )
+    part0 = product_t(grad_qkv, w_qkv)
+    sums = jnp.stack(
+        [
+            jnp.sum(part0 * unit0, 0),
+            jnp.sum(part1 * unit1, 0),
+            jnp.sum(part2 * unit2, 0),
+            jnp.sum(part0, 0),
+            jnp.sum(part1, 0),
+            jnp.sum(part2, 0),
+            0.5 * jnp.sum(wide(grad_encoded), 0),
+            jnp.zeros((D,), jnp.float32),
+        ]
+    )
+    sums = jnp.pad(narrow(sums).reshape(PARTS, 2, D), ((0, 0), (0, 14), (0, 0)))
+    qkv_block = reduce_group(
+        *group_blocks(
+            place,
+            [(normed0, grad_qkv, [(0, 128, 0, 0), (128, 128, 144, 0)])],
+            (288, 384),
+            sums,
+        )
+    )
+    norm0_mine, norm0_other = split_rows(part0)
+    grad_norm0 = norm0_mine + wide(partner(narrow(norm0_other)))
+    unit0_mine, _ = split_rows(unit0)
+    after_self_mine, _ = split_rows(grad_after_self)
+    scale0_mine = lax.dynamic_index_in_dim(
+        scale0.reshape(STAGES, 2, rows, 1), core, 1, keepdims=False
+    )
+    grad_inputs = after_self_mine + normal_back(unit0_mine, scale0_mine, gains[0], grad_norm0)
+    long_input_grad, short_input_grad = back_to_frames(grad_inputs)
+
+    shard = D // 8
+    (feed_out_grad,) = finish(
+        place, feed_out_block, [(feed_out.shape, [(..., 256, lambda part: part * 256)])]
+    )
+
+    def interleaved(width):
+        return [
+            ((side,), width, lambda part, side=side: (2 * part + side) * width) for side in range(2)
+        ]
+
+    (feed_in_grad,) = finish(place, own_rows(feed_in_block), [(feed_in.shape, interleaved(512))])
+    sides = own_rows(
+        middle_block[2 * shard :].reshape(2, 2, shard, 256).transpose(1, 0, 2, 3).reshape(4 * shard, 256)
+    )
+    sides = sides.reshape(4 * shard, 256)
+    middle_block = jnp.concatenate([middle_block[: 2 * shard], sides], 0)
+
+    def rows_at(first, count=shard, lanes=slice(None)):
+        return (slice(first, first + count), lanes)
+
+    cross_out_grad, self_out_grad, cross_query_grad, text_proj_grad, cross_keyval_grad = finish(
+        place,
+        middle_block,
+        [
+            (cross_out.shape, [(rows_at(0), 256, lambda part: part * 256)]),
+            (self_out.shape, [(rows_at(shard), 256, lambda part: part * 256)]),
+            (
+                cross_query.shape,
+                [
+                    (
+                        rows_at((2 + 2 * side) * shard, shard, slice(0, 128)),
+                        128,
+                        lambda part, side=side: (2 * part + side) * 128,
+                    )
+                    for side in range(2)
+                ],
+            ),
+            (
+                text_proj.shape,
+                [
+                    (
+                        rows_at((2 + 2 * side) * shard, text_rows, slice(128, 256)),
+                        128,
+                        lambda part, side=side: side * half + part * 128,
+                    )
+                    for side in range(2)
+                ],
+            ),
+            (
+                cross_keyval.shape,
+                [
+                    (
+                        rows_at((3 + 2 * side) * shard, shard, slice(128 * j, 128 * j + 128)),
+                        128,
+                        lambda part, side=side, j=j: (2 * (2 * part + j) + side) * 128,
+                    )
+                    for side in range(2)
+                    for j in range(2)
+                ],
+            ),
+        ],
+    )
+    qkv_grad, sums = finish(
+        place,
+        own_rows(qkv_block),
+        [
+            (
+                qkv_weight.shape,
+                [
+                    (
+                        (side, slice(0, shard), slice(128 * j, 128 * j + 128)),
+                        128,
+                        lambda part, side=side, j=j: (2 * (3 * part + j) + side) * 128,
+                    )
+                    for side in range(2)
+                    for j in range(3)
+                ],
+            )
+        ],
+        True,
+    )
+    sums = sums[:, :2].reshape(8, shard)
+    return (
+        long_output,
+        short_output,
+        wide(long_input_grad),
+        wide(short_input_grad),
+        long_text_grad,
+        short_text_grad,
+        qkv_grad,
+        self_out_grad,
+        cross_query_grad,
+        cross_keyval_grad,
+        cross_out_grad,
+        text_proj_grad,
+        sums[6],
+        feed_in_grad,
+        feed_out_grad,
+        sums[0:3],
+        sums[3:6],
+    )
+
+
 def solution(mesh):
     return jax.shard_map(
-        on_device,
+        on_item_device if fits_item_plan(mesh) else on_device,
         mesh=mesh,
         in_specs=(
             P("dp", "seq", None),

time: 1270 us -> 551 us (0.43)
  waiting for transfers between devices: 830 us -> 185 us
  matrix products: 165 us -> 48.6 us
  Pallas kernels: 0 us -> 109 us
  blocking collectives: 71.1 us -> 0 us
  local copies, waits for them, and re-layouts: 80.6 us -> 30.9 us
  other arithmetic: 32.7 us -> 73.8 us
  starting transfers between devices: 64.3 us -> 90.4 us
  between operations: 17.7 us -> 3.01 us
    reduce_scatter x8 -> x0, waiting for transfers between devices: 276 us -> none  [the longest x1 90.2 us: on_device(): lax.psum_scatter(grads[7].astype(jnp.bfloat16), 'seq', scatter_dimension=...]
    all_to_all x16 -> x5, waiting for transfers between devices: 202 us -> 18.7 us  [stage_exchange(): lax.all_to_all(blocks, 'seq', split_axis=0, concat_axis=0, axis_index_gro...]
    all_gather x8 -> x0, waiting for transfers between devices: 171 us -> none  [the longest x1 65.3 us: on_device(): lax.all_gather(feed_out, 'seq', axis=0, tiled=True)]
    ppermute x0 -> x72, waiting for transfers between devices: none -> 166 us  [the longest x24 90.5 us: next_stage(): lax.ppermute(values, 'seq', [(rank, (rank + 2) % count) for rank in range...]
    pallas_call x0 -> x22, Pallas kernels: none -> 109 us  [the longest x2 31.6 us: attend_back_pair(): pl.pallas_call(partial(attend_back_kernel, causal), out_shape=[jax.ShapeD...]
    psum x1 -> x0, waiting for transfers between devices: 100 us -> none  [on_device(): lax.psum(shares[0].astype(jnp.bfloat16), 'dp').astype(jnp.float32)]
    unnamed x25 -> x0, waiting for transfers between devices: 81.7 us -> none
    dot_general x32 -> x0, matrix products: 72.8 us -> none  [the longest x6 31.9 us: weight_grad(): lax.dot_general(left, right, (((0,), (0,)), ((), ())), preferred_element_...]
  transfers between devices with their start and end apart: 37 -> 77, of which waited for: 28 -> 34; matrix products, arithmetic and copies ran while one was open for 19% -> 18% of each run, Pallas kernels for 0% -> 18%
where the time goes in v1:
time: 551 us; the launch traced here: 540 us
  waiting for transfers between devices  185 us (34%)
  Pallas kernels  109 us (20%)
  starting transfers between devices  90.4 us (16%)
  other arithmetic  73.8 us (13%)
  matrix products  48.6 us (9%)
  local copies, waits for them, and re-layouts  30.9 us (6%)
    ppermute x24, waiting for transfers between devices, next_stage(): lax.ppermute(values, 'seq', [(rank, (rank + 2) % count) for rank in range...  90.5 us
    ppermute x32, waiting for transfers between devices, across(): return lax.ppermute(values, ALL_AXES, pairs)  72.6 us
    ppermute x32, starting transfers between devices, across(): return lax.ppermute(values, ALL_AXES, pairs)  35.7 us
    dot_general x8, matrix products, product_t(): lax.dot_general(left, right, (((left.ndim - 1,), (1,)), ((), ())), prefer...  31.8 us
    pallas_call x2, Pallas kernels, attend_back_pair(): pl.pallas_call(partial(attend_back_kernel, causal), out_shape=[jax.ShapeD...  31.6 us
    convert_element_type x25, other arithmetic, narrow(): return values.astype(jnp.bfloat16)  31.5 us
    pallas_call x4, Pallas kernels, group_blocks(): pl.pallas_call(kernel, out_shape=[jax.ShapeDtypeStruct((2, STAGES, *shape...  31 us
    ppermute x24, starting transfers between devices, next_stage(): lax.ppermute(values, 'seq', [(rank, (rank + 2) % count) for rank in range...  26.7 us
  transfers between devices with their start and end apart: 77, of which 34 were waited for; matrix products, arithmetic and copies ran while one was open for 18% of the time, Pallas kernels for 18%

profile of v1, /device:TPU:0, one launch (start us, length us, event | category | flops | bytes accessed | tf_op | source)
XLA Modules:
  0.0 540.4 jit_solution(17692279598112570681)
XLA Ops:
  16.3 4.3 all-to-all-start
  23.1 19.2 %collective-permute-done.3 = bf16[192,512]{1,0:T(8,128)(2,1)S(1)} collective-permute-done((bf16[192,512]{1,0:T(8,128)(2,1)}, bf16[192,512]{1,0:T(8,128)(2,1)S(1)}, u32[]{:S(2)}, u32[]{:S(2)}) %collective-permute-start.3) | collective-permute-done | bytes 196640 | tf_op jit(solution)/shard_map/ppermute | solution.py:439
  47.7 3.8 collective-permute-done.4
  54.1 4.2 collective-permute-done.9
  60.0 3.4 collective-permute-done.5.refs_1_
  64.9 4.9 collective-permute-done.10
  93.0 16.5 %collective-permute-done.12.refs_1_ = bf16[3,368,512]{2,1,0:T(8,128)(2,1)} collective-permute-done((bf16[3,368,512]{2,1,0:T(8,128)(2,1)}, bf16[3,368,512]{2,1,0:T(8,128)(2,1)}, u32[]{:S(2)}, u32[]{:S(2)}) %collective-permute-start.12) | collective-permute-done | bytes 1130528 | tf_op jit(solution)/shard_map/ppermute | solution.py:448
  112.1 3.7 copy.61
  118.4 5.9 %collective-permute-done.19 = bf16[256,512]{1,0:T(8,128)(2,1)} collective-permute-done((bf16[256,512]{1,0:T(8,128)(2,1)S(1)}, bf16[256,512]{1,0:T(8,128)(2,1)}, u32[]{:S(2)}, u32[]{:S(2)}) %collective-permute-start.19) | collective-permute-done | bytes 262176 | tf_op jit(solution)/shard_map/ppermute | solution.py:439
  127.5 14.7 %shard_map.326.refs_2_ = bf16[640,512]{1,0:T(8,128)(2,1)S(1)} custom-call(f32[1,640]{1,0:T(1,128)S(1)} %and_convert_fusion.valid_ref, bf16[640,1536]{1,0:T(8,128)(2,1)S(1)} %convolution_convert_fusion.q_ref.k_ref.v_ref, bf16[640,1536]{1,0:T(8,128)(2,1)S(1)} %convolution_convert_fusion.q_ref.k_ref.v_ref, ...), custom_call_target="tpu_custom_call" | custom-call | tf_op jit(solution)/shard_map/pallas_call | solution.py:828
  144.0 4.0 shard_map.329
  149.1 3.2 fusion.91
  155.1 3.4 collective-permute-start.26
  162.0 4.4 all-to-all-start.2
  177.2 4.2 shard_map.330.refs_0_
  189.7 8.5 %collective-permute-done.23.refs_3_ = bf16[3,256,512]{2,1,0:T(8,128)(2,1)} collective-permute-done((bf16[3,256,512]{2,1,0:T(8,128)(2,1)}, bf16[3,256,512]{2,1,0:T(8,128)(2,1)}, u32[]{:S(2)}, u32[]{:S(2)}) %collective-permute-start.23) | collective-permute-done | bytes 786464 | tf_op jit(solution)/shard_map/ppermute | solution.py:448
  206.5 8.4 %collective-permute-done.29.refs_3_ = bf16[3,256,512]{2,1,0:T(8,128)(2,1)S(1)} collective-permute-done((bf16[3,256,512]{2,1,0:T(8,128)(2,1)}, bf16[3,256,512]{2,1,0:T(8,128)(2,1)S(1)}, u32[]{:S(2)}, u32[]{:S(2)}) %collective-permute-start.29) | collective-permute-done | bytes 786464 | tf_op jit(solution)/shard_map/ppermute | solution.py:448
  224.0 16.2 %add_convert_fusion = (bf16[640,2048]{1,0:T(8,128)(2,1)S(1)}, f32[640,2048]{1,0:T(8,128)}) fusion(f32[640,2048]{1,0:T(8,128)S(1)} %fusion.96, bf16[640,1024]{1,0:T(8,128)(2,1)S(1)} %bitcast.300, bf16[2048,1024]{1,0:T(8,128)(2,1)S(1)} %shard_map.334), kind=kOutput, calls=%fused_computation.2 | convolution fusion | flops 2778726400 | bytes 18612224 | tf_op jit(solution)/shard_map/dot_general | solution.py:37
  240.2 4.8 fusion.93
  245.0 5.5 %multiply_convert_fusion.refs_0_ = bf16[640,2048]{1,0:T(8,128)(2,1)S(1)} fusion(f32[640,2048]{1,0:T(8,128)} %get-tuple-element.108, f32[640,2048]{1,0:T(8,128)} %copy-done.68), kind=kLoop, calls=%fused_computation.3 | loop fusion | flops 3932160 | bytes 13107200 | tf_op jit(solution)/shard_map/convert_element_type | solution.py:742
  250.6 4.2 multiply_reduce_fusion
  254.8 3.6 fusion.84
  259.9 7.1 %shard_map.335 = (bf16[640,512]{1,0:T(8,128)(2,1)S(1)}, bf16[64,512]{1,0:T(8,128)(2,1)S(1)}, bf16[64,512]{1,0:T(8,128)(2,1)S(1)}) custom-call(f32[1,64]{1,0:T(1,128)S(1)} %compare_convert_fusion.valid_ref, bf16[640,512]{1,0:T(8,128)(2,1)S(1)} %copy-done.26, bf16[64,1024]{1,0:T(8,128)(2,1)S(1)} %convolution_convert_fusion.4.k_ref.v_ref, ...), custom_call_target="tpu_custom_call" | custom-call | tf_op jit(solution)/shard_map/pallas_call | solution.py:871
  271.3 8.9 %shard_map.343 = (bf16[2,4,512,256]{3,2,1,0:T(8,128)(2,1)}, bf16[2,4,512,256]{3,2,1,0:T(8,128)(2,1)S(1)}) custom-call(s32[3]{0:T(128)S(1)} %pad_add_fusion.place_ref, bf16[640,2048]{1,0:T(8,128)(2,1)} %copy-done.65, bf16[640,1024]{1,0:T(8,128)(2,1)S(1)} %bitcast.301), custom_call_target="tpu_custom_call" | custom-call | tf_op jit(solution)/shard_map/pallas_call | solution.py:728
  281.5 7.7 %shard_map.341 = (bf16[2,4,256,512]{3,2,1,0:T(8,128)(2,1)}, bf16[2,4,256,512]{3,2,1,0:T(8,128)(2,1)S(1)}) custom-call(s32[3]{0:T(128)S(1)} %pad_add_fusion.place_ref, bf16[640,1024]{1,0:T(8,128)(2,1)S(1)} %copy-done.13, bf16[640,2048]{1,0:T(8,128)(2,1)} %copy-done.73), custom_call_target="tpu_custom_call" | custom-call | tf_op jit(solution)/shard_map/pallas_call | solution.py:728
  294.2 5.1 all-to-all-start.4
  305.0 4.4 all-to-all-start.1
  309.4 4.1 fusion.94
  314.2 11.6 %all-to-all-done.1 = bf16[4,80,1024]{2,1,0:T(8,128)(2,1)} async-done(((bf16[4,80,1024]{2,1,0:T(8,128)(2,1)}), bf16[4,80,1024]{2,1,0:T(8,128)(2,1)}, u32[]{:S(2)}, u32[]{:S(2)}) %all-to-all-start.1) | async-done | bytes 655392 | tf_op jit(solution)/shard_map/all_to_all | solution.py:453
  332.9 8.9 %collective-permute-done.55 = bf16[2,4,256,512]{3,2,1,0:T(8,128)(2,1)} collective-permute-done((bf16[2,4,256,512]{3,2,1,0:T(8,128)(2,1)}, bf16[2,4,256,512]{3,2,1,0:T(8,128)(2,1)}, u32[]{:S(2)}, u32[]{:S(2)}) %collective-permute-start.55) | collective-permute-done | bytes 2097184 | tf_op jit(solution)/shard_map/ppermute | solution.py:448
  347.6 3.5 fusion.83
  352.9 9.1 %shard_map.339 = (bf16[2,4,768,256]{3,2,1,0:T(8,128)(2,1)}, bf16[2,4,768,256]{3,2,1,0:T(8,128)(2,1)}) custom-call(s32[3]{0:T(128)S(1)} %pad_add_fusion.place_ref, bf16[640,512]{1,0:T(8,128)(2,1)S(1)} %copy-done.9, bf16[640,1024]{1,0:T(8,128)(2,1)S(1)} %copy-done.15, bf16[640,512]{1,0:T(8,128)(2,1)S(1)} %copy-done.7, ...), custom_call_target="tpu_custom_call" | custom-call | tf_op jit(solution)/shard_map/pallas_call | solution.py:728
  363.4 24.5 %shard_map.336 = (bf16[640,512]{1,0:T(8,128)(2,1)S(1)}, bf16[640,512]{1,0:T(8,128)(2,1)S(1)}, bf16[640,512]{1,0:T(8,128)(2,1)S(1)}) custom-call(f32[1,640]{1,0:T(1,128)S(1)} %and_convert_fusion.valid_ref, bf16[640,1536]{1,0:T(8,128)(2,1)S(1)} %convolution_convert_fusion.q_ref.k_ref.v_ref, bf16[640,1536]{1,0:T(8,128)(2,1)S(1)} %convolution_convert_fusion.q_ref.k_ref.v_ref, ...), custom_call_target="tpu_custom_call" | custom-call | tf_op jit(solution)/shard_map/pallas_call | solution.py:871
  390.5 3.8 fusion.82
  394.5 5.3 shard_map.337
  404.2 6.1 %collective-permute-start.66 = (bf16[512,256]{1,0:T(8,128)(2,1)S(1)}, bf16[512,256]{1,0:T(8,128)(2,1)S(1)}, u32[]{:S(2)}, u32[]{:S(2)}) collective-permute-start(bf16[512,256]{1,0:T(8,128)(2,1)S(1)} %fusion.57), channel_id=1, source_target_pairs={{0,2},{1,3},{2,4},{3,5},{4,6},{5,7},{6,0},{7,1},{8,10},{9,11},{10,... | collective-permute-start | bytes 786440 | tf_op jit(solution)/shard_map/ppermute | solution.py:439
  413.9 4.7 collective-permute-done.66
  419.6 4.6 collective-permute-done.57
  431.1 4.3 collective-permute-done.58
  436.5 4.8 collective-permute-done.68
  442.9 14.1 %collective-permute-done.38 = bf16[4,288,384]{2,1,0:T(8,128)(2,1)S(1)} collective-permute-done((bf16[4,288,384]{2,1,0:T(8,128)(2,1)S(1)}, bf16[4,288,384]{2,1,0:T(8,128)(2,1)S(1)}, u32[]{:S(2)}, u32[]{:S(2)}) %collective-permute-start.38) | collective-permute-done | bytes 884768 | tf_op jit(solution)/shard_map/ppermute | solution.py:448
  461.8 5.6 %collective-permute-done.39 = bf16[288,384]{1,0:T(8,128)(2,1)S(1)} collective-permute-done((bf16[288,384]{1,0:T(8,128)(2,1)S(1)}, bf16[288,384]{1,0:T(8,128)(2,1)S(1)}, u32[]{:S(2)}, u32[]{:S(2)}) %collective-permute-start.39) | collective-permute-done | bytes 221216 | tf_op jit(solution)/shard_map/ppermute | solution.py:439
  467.6 8.3 %collective-permute-done.48 = bf16[768,256]{1,0:T(8,128)(2,1)S(1)} collective-permute-done((bf16[768,256]{1,0:T(8,128)(2,1)S(1)}, bf16[768,256]{1,0:T(8,128)(2,1)S(1)}, u32[]{:S(2)}, u32[]{:S(2)}) %collective-permute-start.48) | collective-permute-done | bytes 393248 | tf_op jit(solution)/shard_map/ppermute | solution.py:439
  480.7 9.1 %collective-permute-done.49 = bf16[768,256]{1,0:T(8,128)(2,1)S(1)} collective-permute-done((bf16[768,256]{1,0:T(8,128)(2,1)S(1)}, bf16[768,256]{1,0:T(8,128)(2,1)S(1)}, u32[]{:S(2)}, u32[]{:S(2)}) %collective-permute-start.49) | collective-permute-done | bytes 393248 | tf_op jit(solution)/shard_map/ppermute | solution.py:439
  491.4 5.1 all-to-all-start.3
  509.0 4.5 all-to-all-done.3
  528.7 4.6 collective-permute-done.53.refs_2_
  533.3 4.2 collective-permute-done.54.refs_3_
  (474 shorter events, 202.4 us)
Async XLA Ops:
  10.9 33.4 %collective-permute-start.8 = (bf16[992,512]{1,0:T(8,128)(2,1)}, bf16[992,512]{1,0:T(8,128)(2,1)S(1)}, u32[]{:S(2)}, u32[]{:S(2)}) collective-permute-start(bf16[992,512]{1,0:T(8,128)(2,1)} %get-tuple-element.58), channel_id=1, source_target_pairs={{0,1},{1,0},{2,3},{3,2},{4,5},{5,4},{6,7},{7,6},{8,9},{9,8},{10,11... | collective-permute-start | bytes 3047432 | tf_op jit(solution)/shard_map/ppermute | solution.py:434
  16.3 42.1 %all-to-all-start = ((bf16[4,96,1024]{2,1,0:T(8,128)(2,1)}), bf16[4,96,1024]{2,1,0:T(8,128)(2,1)}, u32[]{:S(2)}, u32[]{:S(2)}) async-start(bf16[4,96,1024]{2,1,0:T(8,128)(2,1)} %fusion.25), calls=%async_computation | async-start | bytes 1572864 | tf_op jit(solution)/shard_map/all_to_all | solution.py:453
  23.1 19.2 %collective-permute-start.3 = (bf16[192,512]{1,0:T(8,128)(2,1)}, bf16[192,512]{1,0:T(8,128)(2,1)S(1)}, u32[]{:S(2)}, u32[]{:S(2)}) collective-permute-start(bf16[192,512]{1,0:T(8,128)(2,1)} %collective-permute-done.2), channel_id=1, source_target_pairs={{0,2},{1,3},{2,4},{3,5},{4,6},{5,7},{6,0},{7,1},{8,10},{9,11},{10,... | collective-permute-start | bytes 589832 | tf_op jit(solution)/shard_map/ppermute | solution.py:439
  45.3 13.0 %collective-permute-start.9 = (bf16[368,512]{1,0:T(8,128)(2,1)S(1)}, bf16[368,512]{1,0:T(8,128)(2,1)}, u32[]{:S(2)}, u32[]{:S(2)}) collective-permute-start(bf16[368,512]{1,0:T(8,128)(2,1)S(1)} %shard_map.328), channel_id=1, source_target_pairs={{0,2},{1,3},{2,4},{3,5},{4,6},{5,7},{6,0},{7,1},{8,10},{9,11},{10,... | collective-permute-start | bytes 1130504 | tf_op jit(solution)/shard_map/ppermute | solution.py:439
  58.5 27.5 %collective-permute-start.1 = (bf16[4,96,1024]{2,1,0:T(8,128)(2,1)}, bf16[4,96,1024]{2,1,0:T(8,128)(2,1)}, u32[]{:S(2)}, u32[]{:S(2)}) collective-permute-start(bf16[4,96,1024]{2,1,0:T(8,128)(2,1)} %all-to-all-done), channel_id=1, source_target_pairs={{0,1},{1,0},{2,3},{3,2},{4,5},{5,4},{6,7},{7,6},{8,9},{9,8},{10,11... | collective-permute-start | bytes 2359304 | tf_op jit(solution)/shard_map/ppermute | solution.py:434
  58.5 17.2 %collective-permute-start.6 = (bf16[3,192,512]{2,1,0:T(8,128)(2,1)S(1)}, bf16[3,192,512]{2,1,0:T(8,128)(2,1)}, u32[]{:S(2)}, u32[]{:S(2)}) collective-permute-start(bf16[3,192,512]{2,1,0:T(8,128)(2,1)S(1)} %pad_maximum_fusion.4.refs_0_), channel_id=1, source_target_pairs={{0,16},{1,9},{2,18},{3,11},{4,20},{5,13},{6,22},{7,15},{8,24},{9,1... | collective-permute-start | bytes 1769480 | tf_op jit(solution)/shard_map/ppermute | solution.py:448
  75.3 40.6 %collective-permute-start.18 = (bf16[256,512]{1,0:T(8,128)(2,1)S(1)}, bf16[256,512]{1,0:T(8,128)(2,1)S(1)}, u32[]{:S(2)}, u32[]{:S(2)}) collective-permute-start(bf16[256,512]{1,0:T(8,128)(2,1)S(1)} %shard_map.331), channel_id=1, source_target_pairs={{0,2},{1,3},{2,4},{3,5},{4,6},{5,7},{6,0},{7,1},{8,10},{9,11},{10,... | collective-permute-start | bytes 786440 | tf_op jit(solution)/shard_map/ppermute | solution.py:439
  84.5 25.0 %collective-permute-start.12 = (bf16[3,368,512]{2,1,0:T(8,128)(2,1)}, bf16[3,368,512]{2,1,0:T(8,128)(2,1)}, u32[]{:S(2)}, u32[]{:S(2)}) collective-permute-start(bf16[3,368,512]{2,1,0:T(8,128)(2,1)} %pad_maximum_fusion.1.refs_0_), channel_id=1, source_target_pairs={{0,8},{1,17},{2,10},{3,19},{4,12},{5,21},{6,14},{7,23},{8,0},{9,25... | collective-permute-start | bytes 3391496 | tf_op jit(solution)/shard_map/ppermute | solution.py:448
  91.5 52.5 %collective-permute-start.13 = (bf16[3,368,512]{2,1,0:T(8,128)(2,1)}, bf16[3,368,512]{2,1,0:T(8,128)(2,1)}, u32[]{:S(2)}, u32[]{:S(2)}) collective-permute-start(bf16[3,368,512]{2,1,0:T(8,128)(2,1)} %pad_maximum_fusion.1.refs_0_), channel_id=1, source_target_pairs={{0,16},{1,9},{2,18},{3,11},{4,20},{5,13},{6,22},{7,15},{8,24},{9,1... | collective-permute-start | bytes 3391496 | tf_op jit(solution)/shard_map/ppermute | solution.py:448
  109.5 34.5 %collective-permute-start.14 = (bf16[3,368,512]{2,1,0:T(8,128)(2,1)}, bf16[3,368,512]{2,1,0:T(8,128)(2,1)}, u32[]{:S(2)}, u32[]{:S(2)}) collective-permute-start(bf16[3,368,512]{2,1,0:T(8,128)(2,1)} %collective-permute-done.12.refs_1_), channel_id=1, source_target_pairs={{0,16},{1,9},{2,18},{3,11},{4,20},{5,13},{6,22},{7,15},{8,24},{9,1... | collective-permute-start | bytes 3391496 | tf_op jit(solution)/shard_map/ppermute | solution.py:448
  124.3 19.7 %collective-permute-start.24 = (bf16[256,512]{1,0:T(8,128)(2,1)}, bf16[256,512]{1,0:T(8,128)(2,1)}, u32[]{:S(2)}, u32[]{:S(2)}) collective-permute-start(bf16[256,512]{1,0:T(8,128)(2,1)} %shard_map.333), channel_id=1, source_target_pairs={{0,2},{1,3},{2,4},{3,5},{4,6},{5,7},{6,0},{7,1},{8,10},{9,11},{10,... | collective-permute-start | bytes 786440 | tf_op jit(solution)/shard_map/ppermute | solution.py:439
  142.3 16.1 %collective-permute-start.20 = (bf16[256,512]{1,0:T(8,128)(2,1)}, bf16[256,512]{1,0:T(8,128)(2,1)}, u32[]{:S(2)}, u32[]{:S(2)}) collective-permute-start(bf16[256,512]{1,0:T(8,128)(2,1)} %collective-permute-done.19), channel_id=1, source_target_pairs={{0,2},{1,3},{2,4},{3,5},{4,6},{5,7},{6,0},{7,1},{8,10},{9,11},{10,... | collective-permute-start | bytes 786440 | tf_op jit(solution)/shard_map/ppermute | solution.py:439
  152.3 18.9 %collective-permute-start.15 = (bf16[640,1024]{1,0:T(8,128)(2,1)}, bf16[640,1024]{1,0:T(8,128)(2,1)}, u32[]{:S(2)}, u32[]{:S(2)}) collective-permute-start(bf16[640,1024]{1,0:T(8,128)(2,1)} %get-tuple-element.140), channel_id=1, source_target_pairs={{0,1},{1,0},{2,3},{3,2},{4,5},{5,4},{6,7},{7,6},{8,9},{9,8},{10,11... | collective-permute-start | bytes 3932168 | tf_op jit(solution)/shard_map/ppermute | solution.py:434
  155.1 13.0 %collective-permute-start.26 = (bf16[256,512]{1,0:T(8,128)(2,1)}, bf16[256,512]{1,0:T(8,128)(2,1)S(1)}, u32[]{:S(2)}, u32[]{:S(2)}) collective-permute-start(bf16[256,512]{1,0:T(8,128)(2,1)} %collective-permute-done.25), channel_id=1, source_target_pairs={{0,2},{1,3},{2,4},{3,5},{4,6},{5,7},{6,0},{7,1},{8,10},{9,11},{10,... | collective-permute-start | bytes 786440 | tf_op jit(solution)/shard_map/ppermute | solution.py:439
  160.5 25.3 %collective-permute-start.21 = (bf16[3,256,512]{2,1,0:T(8,128)(2,1)}, bf16[3,256,512]{2,1,0:T(8,128)(2,1)}, u32[]{:S(2)}, u32[]{:S(2)}) collective-permute-start(bf16[3,256,512]{2,1,0:T(8,128)(2,1)} %pad_maximum_fusion.2.refs_0_), channel_id=1, source_target_pairs={{0,8},{1,17},{2,10},{3,19},{4,12},{5,21},{6,14},{7,23},{8,0},{9,25... | collective-permute-start | bytes 2359304 | tf_op jit(solution)/shard_map/ppermute | solution.py:448
  162.0 24.3 %collective-permute-start.22 = (bf16[3,256,512]{2,1,0:T(8,128)(2,1)}, bf16[3,256,512]{2,1,0:T(8,128)(2,1)}, u32[]{:S(2)}, u32[]{:S(2)}) collective-permute-start(bf16[3,256,512]{2,1,0:T(8,128)(2,1)} %pad_maximum_fusion.2.refs_0_), channel_id=1, source_target_pairs={{0,16},{1,9},{2,18},{3,11},{4,20},{5,13},{6,22},{7,15},{8,24},{9,1... | collective-permute-start | bytes 2359304 | tf_op jit(solution)/shard_map/ppermute | solution.py:448
  162.0 24.2 %all-to-all-start.2 = ((bf16[4,80,1024]{2,1,0:T(8,128)(2,1)}), bf16[4,80,1024]{2,1,0:T(8,128)(2,1)}, u32[]{:S(2)}, u32[]{:S(2)}) async-start(bf16[4,80,1024]{2,1,0:T(8,128)(2,1)} %fusion.34), calls=%async_computation.2 | async-start | bytes 1310720 | tf_op jit(solution)/shard_map/all_to_all | solution.py:453
  170.1 18.7 %collective-permute-start.27 = (bf16[3,256,512]{2,1,0:T(8,128)(2,1)}, bf16[3,256,512]{2,1,0:T(8,128)(2,1)}, u32[]{:S(2)}, u32[]{:S(2)}) collective-permute-start(bf16[3,256,512]{2,1,0:T(8,128)(2,1)} %pad_maximum_fusion.3.refs_0_), channel_id=1, source_target_pairs={{0,8},{1,17},{2,10},{3,19},{4,12},{5,21},{6,14},{7,23},{8,0},{9,25... | collective-permute-start | bytes 2359304 | tf_op jit(solution)/shard_map/ppermute | solution.py:448
  184.2 33.1 %collective-permute-start.17 = (bf16[640,1024]{1,0:T(8,128)(2,1)}, bf16[640,1024]{1,0:T(8,128)(2,1)}, u32[]{:S(2)}, u32[]{:S(2)}) collective-permute-start(bf16[640,1024]{1,0:T(8,128)(2,1)} %get-tuple-element.142), channel_id=1, source_target_pairs={{0,1},{1,0},{2,3},{3,2},{4,5},{5,4},{6,7},{7,6},{8,9},{9,8},{10,11... | collective-permute-start | bytes 3932168 | tf_op jit(solution)/shard_map/ppermute | solution.py:434
  186.3 16.1 %collective-permute-start.31 = (bf16[4,80,1024]{2,1,0:T(8,128)(2,1)}, bf16[4,80,1024]{2,1,0:T(8,128)(2,1)S(1)}, u32[]{:S(2)}, u32[]{:S(2)}) collective-permute-start(bf16[4,80,1024]{2,1,0:T(8,128)(2,1)} %all-to-all-done.2), channel_id=1, source_target_pairs={{0,1},{1,0},{2,3},{3,2},{4,5},{5,4},{6,7},{7,6},{8,9},{9,8},{10,11... | collective-permute-start | bytes 1966088 | tf_op jit(solution)/shard_map/ppermute | solution.py:434
  186.3 20.2 %collective-permute-start.28 = (bf16[3,256,512]{2,1,0:T(8,128)(2,1)}, bf16[3,256,512]{2,1,0:T(8,128)(2,1)S(1)}, u32[]{:S(2)}, u32[]{:S(2)}) collective-permute-start(bf16[3,256,512]{2,1,0:T(8,128)(2,1)} %pad_maximum_fusion.3.refs_0_), channel_id=1, source_target_pairs={{0,16},{1,9},{2,18},{3,11},{4,20},{5,13},{6,22},{7,15},{8,24},{9,1... | collective-permute-start | bytes 2359304 | tf_op jit(solution)/shard_map/ppermute | solution.py:448
  188.8 26.1 %collective-permute-start.29 = (bf16[3,256,512]{2,1,0:T(8,128)(2,1)}, bf16[3,256,512]{2,1,0:T(8,128)(2,1)S(1)}, u32[]{:S(2)}, u32[]{:S(2)}) collective-permute-start(bf16[3,256,512]{2,1,0:T(8,128)(2,1)} %collective-permute-done.27.refs_1_), channel_id=1, source_target_pairs={{0,16},{1,9},{2,18},{3,11},{4,20},{5,13},{6,22},{7,15},{8,24},{9,1... | collective-permute-start | bytes 2359304 | tf_op jit(solution)/shard_map/ppermute | solution.py:448
  267.8 23.6 %collective-permute-start.35 = (bf16[64,1024]{1,0:T(8,128)(2,1)S(1)}, bf16[64,1024]{1,0:T(8,128)(2,1)S(1)}, u32[]{:S(2)}, u32[]{:S(2)}) collective-permute-start(bf16[64,1024]{1,0:T(8,128)(2,1)S(1)} %get-tuple-element.148), channel_id=1, source_target_pairs={{0,1},{1,0},{2,3},{3,2},{4,5},{5,4},{6,7},{7,6},{8,9},{9,8},{10,11... | collective-permute-start | bytes 393224 | tf_op jit(solution)/shard_map/ppermute | solution.py:434
  289.2 40.2 %collective-permute-start.64 = (bf16[2,4,512,256]{3,2,1,0:T(8,128)(2,1)}, bf16[2,4,512,256]{3,2,1,0:T(8,128)(2,1)}, u32[]{:S(2)}, u32[]{:S(2)}) collective-permute-start(bf16[2,4,512,256]{3,2,1,0:T(8,128)(2,1)} %get-tuple-element.88), channel_id=1, source_target_pairs={{0,16},{1,9},{2,18},{3,11},{4,20},{5,13},{6,22},{7,15},{8,24},{9,1... | collective-permute-start | bytes 6291464 | tf_op jit(solution)/shard_map/ppermute | solution.py:448
  289.6 52.1 %collective-permute-start.55 = (bf16[2,4,256,512]{3,2,1,0:T(8,128)(2,1)}, bf16[2,4,256,512]{3,2,1,0:T(8,128)(2,1)}, u32[]{:S(2)}, u32[]{:S(2)}) collective-permute-start(bf16[2,4,256,512]{3,2,1,0:T(8,128)(2,1)} %get-tuple-element.86), channel_id=1, source_target_pairs={{0,16},{1,9},{2,18},{3,11},{4,20},{5,13},{6,22},{7,15},{8,24},{9,1... | collective-permute-start | bytes 6291464 | tf_op jit(solution)/shard_map/ppermute | solution.py:448
  305.0 20.9 %all-to-all-start.1 = ((bf16[4,80,1024]{2,1,0:T(8,128)(2,1)}), bf16[4,80,1024]{2,1,0:T(8,128)(2,1)}, u32[]{:S(2)}, u32[]{:S(2)}) async-start(bf16[4,80,1024]{2,1,0:T(8,128)(2,1)} %fusion.16), calls=%async_computation.1 | async-start | bytes 1310720 | tf_op jit(solution)/shard_map/all_to_all | solution.py:453
  313.5 31.3 %collective-permute-start.33 = (bf16[640,1024]{1,0:T(8,128)(2,1)}, bf16[640,1024]{1,0:T(8,128)(2,1)}, u32[]{:S(2)}, u32[]{:S(2)}) collective-permute-start(bf16[640,1024]{1,0:T(8,128)(2,1)} %get-tuple-element.146), channel_id=1, source_target_pairs={{0,1},{1,0},{2,3},{3,2},{4,5},{5,4},{6,7},{7,6},{8,9},{9,8},{10,11... | collective-permute-start | bytes 3932168 | tf_op jit(solution)/shard_map/ppermute | solution.py:434
  332.3 69.8 %collective-permute-start.65 = (bf16[4,512,256]{2,1,0:T(8,128)(2,1)}, bf16[4,512,256]{2,1,0:T(8,128)(2,1)}, u32[]{:S(2)}, u32[]{:S(2)}) collective-permute-start(bf16[4,512,256]{2,1,0:T(8,128)(2,1)} %fusion.22), channel_id=1, source_target_pairs={{0,8},{1,17},{2,10},{3,19},{4,12},{5,21},{6,14},{7,23},{8,0},{9,25... | collective-permute-start | bytes 3145736 | tf_op jit(solution)/shard_map/ppermute | solution.py:448
  344.2 66.1 %collective-permute-start.56 = (bf16[4,256,512]{2,1,0:T(8,128)(2,1)}, bf16[4,256,512]{2,1,0:T(8,128)(2,1)}, u32[]{:S(2)}, u32[]{:S(2)}) collective-permute-start(bf16[4,256,512]{2,1,0:T(8,128)(2,1)} %fusion.21), channel_id=1, source_target_pairs={{0,8},{1,17},{2,10},{3,19},{4,12},{5,21},{6,14},{7,23},{8,0},{9,25... | collective-permute-start | bytes 3145736 | tf_op jit(solution)/shard_map/ppermute | solution.py:448
  362.0 63.2 %collective-permute-start.46 = (bf16[2,4,768,256]{3,2,1,0:T(8,128)(2,1)}, bf16[2,4,768,256]{3,2,1,0:T(8,128)(2,1)}, u32[]{:S(2)}, u32[]{:S(2)}) collective-permute-start(bf16[2,4,768,256]{3,2,1,0:T(8,128)(2,1)} %get-tuple-element.78), channel_id=1, source_target_pairs={{0,16},{1,9},{2,18},{3,11},{4,20},{5,13},{6,22},{7,15},{8,24},{9,1... | collective-permute-start | bytes 9437192 | tf_op jit(solution)/shard_map/ppermute | solution.py:448
  399.9 28.8 %collective-permute-start.37 = (bf16[2,4,288,384]{3,2,1,0:T(8,128)(2,1)S(1)}, bf16[2,4,288,384]{3,2,1,0:T(8,128)(2,1)S(1)}, u32[]{:S(2)}, u32[]{:S(2)}) collective-permute-start(bf16[2,4,288,384]{3,2,1,0:T(8,128)(2,1)S(1)} %get-tuple-element.75), channel_id=1, source_target_pairs={{0,16},{1,9},{2,18},{3,11},{4,20},{5,13},{6,22},{7,15},{8,24},{9,1... | collective-permute-start | bytes 5308424 | tf_op jit(solution)/shard_map/ppermute | solution.py:448
  404.2 14.4 %collective-permute-start.66 = (bf16[512,256]{1,0:T(8,128)(2,1)S(1)}, bf16[512,256]{1,0:T(8,128)(2,1)S(1)}, u32[]{:S(2)}, u32[]{:S(2)}) collective-permute-start(bf16[512,256]{1,0:T(8,128)(2,1)S(1)} %fusion.57), channel_id=1, source_target_pairs={{0,2},{1,3},{2,4},{3,5},{4,6},{5,7},{6,0},{7,1},{8,10},{9,11},{10,... | collective-permute-start | bytes 786440 | tf_op jit(solution)/shard_map/ppermute | solution.py:439
  427.1 31.0 %collective-permute-start.47 = (bf16[4,768,256]{2,1,0:T(8,128)(2,1)S(1)}, bf16[4,768,256]{2,1,0:T(8,128)(2,1)S(1)}, u32[]{:S(2)}, u32[]{:S(2)}) collective-permute-start(bf16[4,768,256]{2,1,0:T(8,128)(2,1)S(1)} %fusion.7), channel_id=1, source_target_pairs={{0,8},{1,17},{2,10},{3,19},{4,12},{5,21},{6,14},{7,23},{8,0},{9,25... | collective-permute-start | bytes 4718600 | tf_op jit(solution)/shard_map/ppermute | solution.py:448
  428.9 28.2 %collective-permute-start.38 = (bf16[4,288,384]{2,1,0:T(8,128)(2,1)S(1)}, bf16[4,288,384]{2,1,0:T(8,128)(2,1)S(1)}, u32[]{:S(2)}, u32[]{:S(2)}) collective-permute-start(bf16[4,288,384]{2,1,0:T(8,128)(2,1)S(1)} %fusion.23), channel_id=1, source_target_pairs={{0,8},{1,17},{2,10},{3,19},{4,12},{5,21},{6,14},{7,23},{8,0},{9,25... | collective-permute-start | bytes 2654216 | tf_op jit(solution)/shard_map/ppermute | solution.py:448
  435.5 26.1 %collective-permute-start.59 = (bf16[256,512]{1,0:T(8,128)(2,1)S(1)}, bf16[256,512]{1,0:T(8,128)(2,1)S(1)}, u32[]{:S(2)}, u32[]{:S(2)}) collective-permute-start(bf16[256,512]{1,0:T(8,128)(2,1)S(1)} %fusion.46), channel_id=1, source_target_pairs={{0,2},{1,3},{2,4},{3,5},{4,6},{5,7},{6,0},{7,1},{8,10},{9,11},{10,... | collective-permute-start | bytes 786440 | tf_op jit(solution)/shard_map/ppermute | solution.py:439
  441.4 56.5 %collective-permute-start.69 = (bf16[512,256]{1,0:T(8,128)(2,1)S(1)}, bf16[512,256]{1,0:T(8,128)(2,1)S(1)}, u32[]{:S(2)}, u32[]{:S(2)}) collective-permute-start(bf16[512,256]{1,0:T(8,128)(2,1)S(1)} %fusion.42.refs_0_), channel_id=1, source_target_pairs={{0,8},{1,17},{2,10},{3,19},{4,12},{5,21},{6,14},{7,23},{8,0},{9,25... | collective-permute-start | bytes 786440 | tf_op jit(solution)/shard_map/ppermute | solution.py:448
  460.1 15.8 %collective-permute-start.48 = (bf16[768,256]{1,0:T(8,128)(2,1)S(1)}, bf16[768,256]{1,0:T(8,128)(2,1)S(1)}, u32[]{:S(2)}, u32[]{:S(2)}) collective-permute-start(bf16[768,256]{1,0:T(8,128)(2,1)S(1)} %fusion.55), channel_id=1, source_target_pairs={{0,2},{1,3},{2,4},{3,5},{4,6},{5,7},{6,0},{7,1},{8,10},{9,11},{10,... | collective-permute-start | bytes 1179656 | tf_op jit(solution)/shard_map/ppermute | solution.py:439
  461.8 14.3 %collective-permute-start.60 = (bf16[128,512]{1,0:T(8,128)(2,1)S(1)}, bf16[128,512]{1,0:T(8,128)(2,1)S(1)}, u32[]{:S(2)}, u32[]{:S(2)}) collective-permute-start(bf16[128,512]{1,0:T(8,128)(2,1)S(1)} %dynamic-slice_bitcast_fusion), channel_id=1, source_target_pairs={{0,1},{1,0},{2,3},{3,2},{4,5},{5,4},{6,7},{7,6},{8,9},{9,8},{10,11... | collective-permute-start | bytes 393224 | tf_op jit(solution)/shard_map/ppermute | solution.py:434
  467.5 13.1 %collective-permute-start.40 = (bf16[288,384]{1,0:T(8,128)(2,1)S(1)}, bf16[288,384]{1,0:T(8,128)(2,1)S(1)}, u32[]{:S(2)}, u32[]{:S(2)}) collective-permute-start(bf16[288,384]{1,0:T(8,128)(2,1)S(1)} %fusion.50), channel_id=1, source_target_pairs={{0,2},{1,3},{2,4},{3,5},{4,6},{5,7},{6,0},{7,1},{8,10},{9,11},{10,... | collective-permute-start | bytes 663560 | tf_op jit(solution)/shard_map/ppermute | solution.py:439
  476.0 13.9 %collective-permute-start.49 = (bf16[768,256]{1,0:T(8,128)(2,1)S(1)}, bf16[768,256]{1,0:T(8,128)(2,1)S(1)}, u32[]{:S(2)}, u32[]{:S(2)}) collective-permute-start(bf16[768,256]{1,0:T(8,128)(2,1)S(1)} %fusion.27), channel_id=1, source_target_pairs={{0,2},{1,3},{2,4},{3,5},{4,6},{5,7},{6,0},{7,1},{8,10},{9,11},{10,... | collective-permute-start | bytes 1179656 | tf_op jit(solution)/shard_map/ppermute | solution.py:439
  476.1 22.4 %collective-permute-start.61 = (bf16[2,128,512]{2,1,0:T(8,128)(2,1)S(1)}, bf16[2,128,512]{2,1,0:T(8,128)(2,1)S(1)}, u32[]{:S(2)}, u32[]{:S(2)}) collective-permute-start(bf16[2,128,512]{2,1,0:T(8,128)(2,1)S(1)} %pad_maximum_fusion.7.refs_0_), channel_id=1, source_target_pairs={{0,8},{1,17},{2,10},{3,19},{4,12},{5,21},{6,14},{7,23},{8,0},{9,25... | collective-permute-start | bytes 786440 | tf_op jit(solution)/shard_map/ppermute | solution.py:448
  480.7 19.2 %collective-permute-start.41 = (bf16[288,384]{1,0:T(8,128)(2,1)S(1)}, bf16[288,384]{1,0:T(8,128)(2,1)S(1)}, u32[]{:S(2)}, u32[]{:S(2)}) collective-permute-start(bf16[288,384]{1,0:T(8,128)(2,1)S(1)} %fusion.52), channel_id=1, source_target_pairs={{0,2},{1,3},{2,4},{3,5},{4,6},{5,7},{6,0},{7,1},{8,10},{9,11},{10,... | collective-permute-start | bytes 663560 | tf_op jit(solution)/shard_map/ppermute | solution.py:439
  490.0 14.0 %collective-permute-start.50 = (bf16[768,256]{1,0:T(8,128)(2,1)S(1)}, bf16[768,256]{1,0:T(8,128)(2,1)S(1)}, u32[]{:S(2)}, u32[]{:S(2)}) collective-permute-start(bf16[768,256]{1,0:T(8,128)(2,1)S(1)} %fusion.29), channel_id=1, source_target_pairs={{0,2},{1,3},{2,4},{3,5},{4,6},{5,7},{6,0},{7,1},{8,10},{9,11},{10,... | collective-permute-start | bytes 1179656 | tf_op jit(solution)/shard_map/ppermute | solution.py:439
  491.4 22.1 %all-to-all-start.3 = ((bf16[4,80,1024]{2,1,0:T(8,128)(2,1)}), bf16[4,80,1024]{2,1,0:T(8,128)(2,1)}, u32[]{:S(2)}, u32[]{:S(2)}) async-start(bf16[4,80,1024]{2,1,0:T(8,128)(2,1)} %fusion.18), calls=%async_computation.3 | async-start | bytes 1310720 | tf_op jit(solution)/shard_map/all_to_all | solution.py:453
  497.8 23.4 %collective-permute-start.62 = (bf16[2,128,512]{2,1,0:T(8,128)(2,1)S(1)}, bf16[2,128,512]{2,1,0:T(8,128)(2,1)S(1)}, u32[]{:S(2)}, u32[]{:S(2)}) collective-permute-start(bf16[2,128,512]{2,1,0:T(8,128)(2,1)S(1)} %pad_maximum_fusion.7.refs_0_), channel_id=1, source_target_pairs={{0,16},{1,9},{2,18},{3,11},{4,20},{5,13},{6,22},{7,15},{8,24},{9,1... | collective-permute-start | bytes 786440 | tf_op jit(solution)/shard_map/ppermute | solution.py:448
  498.5 16.9 %collective-permute-start.71 = (bf16[512,256]{1,0:T(8,128)(2,1)S(1)}, bf16[512,256]{1,0:T(8,128)(2,1)S(1)}, u32[]{:S(2)}, u32[]{:S(2)}) collective-permute-start(bf16[512,256]{1,0:T(8,128)(2,1)S(1)} %collective-permute-done.69.refs_1_), channel_id=1, source_target_pairs={{0,16},{1,9},{2,18},{3,11},{4,20},{5,13},{6,22},{7,15},{8,24},{9,1... | collective-permute-start | bytes 786440 | tf_op jit(solution)/shard_map/ppermute | solution.py:448
  499.8 21.4 %collective-permute-start.63 = (bf16[2,128,512]{2,1,0:T(8,128)(2,1)S(1)}, bf16[2,128,512]{2,1,0:T(8,128)(2,1)S(1)}, u32[]{:S(2)}, u32[]{:S(2)}) collective-permute-start(bf16[2,128,512]{2,1,0:T(8,128)(2,1)S(1)} %collective-permute-done.61.refs_1_), channel_id=1, source_target_pairs={{0,16},{1,9},{2,18},{3,11},{4,20},{5,13},{6,22},{7,15},{8,24},{9,1... | collective-permute-start | bytes 786440 | tf_op jit(solution)/shard_map/ppermute | solution.py:448
  508.4 18.5 %collective-permute-start.52 = (bf16[768,256]{1,0:T(8,128)(2,1)S(1)}, bf16[768,256]{1,0:T(8,128)(2,1)S(1)}, u32[]{:S(2)}, u32[]{:S(2)}) collective-permute-start(bf16[768,256]{1,0:T(8,128)(2,1)S(1)} %pad_maximum_fusion.5.refs_0_), channel_id=1, source_target_pairs={{0,8},{1,17},{2,10},{3,19},{4,12},{5,21},{6,14},{7,23},{8,0},{9,25... | collective-permute-start | bytes 1179656 | tf_op jit(solution)/shard_map/ppermute | solution.py:448
  (124 other events, 1132.7 us)
